TPU v7x, 128 devices: a whole 4x4x4 slice. The times are simulated.
128 devices in a mesh: pixel: 8 (over x, z_lo), date: 16 (over z_hi, y, core).
Axes of the slice: x: 4, y: 4, z: 4 (z_hi: 2, z_lo: 2; z = z_hi * 2 + z_lo), core: 2. Of those that a mesh axis runs over, the one named last changes fastest.
Arguments:
- raw_echoes: bfloat16 [2, 2048, 4096], P(None, ('pixel', 'date')), may hold values from -6 to 6
- range_phase: float32 [4096], replicated, may hold values from -3.140625 to 3.140625
- azimuth_phase: bfloat16 [4096, 2048], P('pixel'), may hold values from -3.140625 to 3.140625
- archive: bfloat16 [32, 2, 4096, 2048], P('date', None, 'pixel'), may hold values from -6 to 6
- date_order: int32 [32], P('date'), may hold values from 0 to 31, as said below
Outputs:
- coherence: float32 [32, 2, 1024, 128], P('date', None, 'pixel')
Inputs may be any that keep to these rules, and one draw needn't show every extreme that they name: `date_order`: entry block b of 2 entries (positions b * 2 to (b + 1) * 2 - 1) holds each of the slots b * 2 to (b + 1) * 2 - 1 exactly once.
All inputs are finite; a program needn't handle non-finite values.
Results may differ from a plain program's by a relative error of at most 0.0041.
Values may be sent and summed in bfloat16 or wider, within the bound.
No kernel may reach another device: no remote copies, remote signals or barrier semaphores. Data moves between devices by JAX's collectives and lax.ppermute only.
A program may use at most 128 MiB of HBM per device.

v0:
```python
from functools import partial
import math

import jax
import jax.numpy as jnp
import numpy as np
from jax import lax
from jax.experimental import pallas as pl
from jax.experimental.pallas import tpu as pltpu
from jax.sharding import PartitionSpec as P

F32 = jnp.float32
BF16 = jnp.bfloat16
EPSILON = 1e-06
R = 4096
A = 2048
ROWS = 64
LINES = 16
VMEM_BYTES = 50 * 2**20
ALL = ("pixel", "date")
VMEM = pl.BlockSpec(memory_space=pltpu.VMEM)


def cmul(a, b):
    return (a[0] * b[0] - a[1] * b[1], a[0] * b[1] + a[1] * b[0])


def turned(value, k, n, sign):
    if k == 0:
        return value
    re, im = value
    if 8 * k == n:
        return ((re - im) * math.sqrt(0.5), (im + re) * math.sqrt(0.5)) if sign > 0 else (
            (re + im) * math.sqrt(0.5),
            (im - re) * math.sqrt(0.5),
        )
    if 8 * k == 3 * n:
        return ((re + im) * -math.sqrt(0.5), (re - im) * math.sqrt(0.5)) if sign > 0 else (
            (im - re) * math.sqrt(0.5),
            (re + im) * -math.sqrt(0.5),
        )
    angle = sign * 2.0 * math.pi * k / n
    return cmul(value, (math.cos(angle), math.sin(angle)))


def fft(values, sign):
    n = len(values)
    if n == 1:
        return values
    even, odd = fft(values[0::2], sign), fft(values[1::2], sign)
    low, high = [], []
    for k in range(n // 2):
        er, ei = even[k]
        if 4 * k == n:
            tr, ti = odd[k]
            plus, minus = (er - ti, ei + tr), (er + ti, ei - tr)
            low.append(plus if sign > 0 else minus)
            high.append(minus if sign > 0 else plus)
        else:
            tr, ti = turned(odd[k], k, n, sign)
            low.append((er + tr, ei + ti))
            high.append((er - tr, ei - ti))
    return low + high


def split(table):
    table = np.asarray(table, np.float32)
    high = table.astype(BF16)
    low = (table - high.astype(np.float32)).astype(BF16)
    return high, low


def real_form(angle, sign):
    c, s = np.cos(angle), sign * np.sin(angle)
    return np.block([[c, s], [-s, c]])


def range_tables():
    t = np.arange(128)
    angle = 2 * np.pi * np.outer(t, t) / 128
    fwd = np.concatenate(split(real_form(angle, -1)), axis=1)
    bwd = np.concatenate(split(real_form(angle, 1)), axis=1)
    twist = 2 * np.pi * np.outer(np.arange(32), t) / R
    return fwd, bwd, np.stack([np.cos(twist), -np.sin(twist)]).astype(np.float32)


def azimuth_tables():
    s = np.arange(128)
    fwd = np.concatenate(split(real_form(2 * np.pi * np.outer(s, s) / 128, -1).T), axis=1)
    k1 = np.arange(128)[:, None]
    i = np.arange(8)[None, :]
    t0 = np.exp(-2j * np.pi * i * k1 / A)
    t1 = np.exp(-2j * np.pi * (i + 8) * k1 / A)
    w = np.exp(-2j * np.pi * i / 16)
    here = np.stack([t0, -w * t1], axis=-1)
    there = np.stack([t1, w * t0], axis=-1)
    twist = np.stack([here.real, here.imag, there.real, there.imag])
    twist = np.repeat(twist, 64, axis=-1).reshape(4, 128, 8 * 128).astype(np.float32)
    k, lam = np.meshgrid(np.arange(8), np.arange(8), indexing="ij")
    m = (lam + 16 * k).reshape(64)
    beta = np.arange(128)
    columns = [real_form(2 * np.pi * np.outer(m + 8 * par, beta) / 128, 1) for par in (0, 1)]
    bwd_high, bwd_low = split(np.concatenate(columns, axis=1))
    bwd = np.stack([bwd_high, bwd_low])
    last = 2 * np.pi * np.outer(np.arange(16), beta) / A
    return fwd, twist, bwd, np.stack([np.cos(last), np.sin(last)]).astype(np.float32)


def pooling_table():
    return (np.arange(A)[:, None] // 16 == np.arange(128)[None, :]).astype(BF16)


def dot(a, b):
    return jnp.dot(a, b, preferred_element_type=F32)


def halves(x):
    high = x.astype(BF16)
    return high, (x - high.astype(F32)).astype(BF16)


def dot_split(x, table):
    high, low = halves(x)
    n = table.shape[1] // 2
    return dot(high, table[:, :n]) + dot(low, table[:, :n]) + dot(high, table[:, n:])


def range_kernel(raw, phase, twist, fwd, bwd, out, a, b):
    values = [
        (raw[0, :, 128 * q : 128 * q + 128].astype(F32), raw[1, :, 128 * q : 128 * q + 128].astype(F32))
        for q in range(32)
    ]
    for k0, value in enumerate(fft(values, -1)):
        re, im = cmul(value, (twist[0, k0 : k0 + 1, :], twist[1, k0 : k0 + 1, :]))
        a[16 * k0 : 16 * k0 + 16, 0:128] = re
        a[16 * k0 : 16 * k0 + 16, 128:256] = im
    b[...] = dot_split(a[...], fwd)
    angle = phase[...]
    cosine, sine = jnp.cos(angle) * (1.0 / R), jnp.sin(angle) * (1.0 / R)
    for k0 in range(32):
        rows = slice(16 * k0, 16 * k0 + 16)
        re, im = cmul((b[rows, 0:128], b[rows, 128:256]), (cosine[k0 : k0 + 1], sine[k0 : k0 + 1]))
        a[rows, 0:128] = re
        a[rows, 128:256] = im
    b[...] = dot_split(a[...], bwd)
    values = []
    for k0 in range(32):
        rows = slice(16 * k0, 16 * k0 + 16)
        values.append(
            cmul((b[rows, 0:128], b[rows, 128:256]), (twist[0, k0 : k0 + 1, :], -twist[1, k0 : k0 + 1, :]))
        )
    left = lax.broadcasted_iota(jnp.int32, (8, 128), 1) < 64
    for q, value in enumerate(fft(values, 1)):
        for half in range(2):
            parts = []
            for part in value:
                low, high = part[0:8], part[8:16]
                if half == 0:
                    parts.append(jnp.where(left, low, pltpu.roll(high, 64, 1)))
                else:
                    parts.append(jnp.where(left, pltpu.roll(low, 64, 1), high))
            message = jnp.concatenate(parts, axis=0).astype(BF16)
            pixel, core, block = q // 4, (q // 2) % 2, 2 * (q % 2) + half
            for zh in range(2):
                y = (block + 2 * zh) % 4
                out[pixel * 16 + zh * 8 + y * 2 + core] = message


def compress_range(raw, phase):
    fwd, bwd, twist = range_tables()
    return pl.pallas_call(
        range_kernel,
        out_shape=jax.ShapeDtypeStruct((128, 16, 128), BF16),
        in_specs=[VMEM] * 5,
        out_specs=VMEM,
        scratch_shapes=[pltpu.VMEM((512, 256), F32)] * 2,
        compiler_params=pltpu.CompilerParams(vmem_limit_bytes=VMEM_BYTES),
        cost_estimate=pl.CostEstimate(flops=4 * 10**8, bytes_accessed=2 * 10**6, transcendentals=8192),
        name="compress_range",
    )(raw, phase.reshape(128, 32).T, twist, fwd, bwd)


def phase_kernel(where, angle, out):
    for k in range(8):
        block = jnp.concatenate(
            [angle[:, 256 * k : 256 * k + 128], angle[:, 256 * k + 128 : 256 * k + 256]], axis=0
        )
        turned_block = block.astype(F32).T
        out[0, k] = jnp.cos(turned_block) * (1.0 / A)
        out[1, k] = jnp.sin(turned_block) * (1.0 / A)


def phase_factors(azimuth_phase, where):
    return pl.pallas_call(
        phase_kernel,
        out_shape=jax.ShapeDtypeStruct((2, 8, 128, 128), F32),
        grid_spec=pltpu.PrefetchScalarGridSpec(
            num_scalar_prefetch=1,
            grid=(1,),
            in_specs=[pl.BlockSpec((ROWS, A), lambda g, where: (where[0], 0))],
            out_specs=pl.BlockSpec((2, 8, 128, 128), lambda g, where: (0, 0, 0, 0)),
        ),
        compiler_params=pltpu.CompilerParams(vmem_limit_bytes=VMEM_BYTES),
        cost_estimate=pl.CostEstimate(flops=10**7, bytes_accessed=2 * 10**6, transcendentals=262144),
        name="phase_factors",
    )(where, azimuth_phase)


def focus_kernel(lines, factors, fwd, twist, bwd, last, out, wide, packed, spec, filtered, parts):
    wide[...] = lines[...].reshape(2048, 128).astype(F32)
    for j in range(16):
        ri, i = j // 8, j % 8
        packed[128 * ri : 128 * ri + 128, 128 * i : 128 * i + 128] = wide[pl.ds(j, 128, stride=16), :].astype(BF16)
    spec[...] = dot(fwd[:, 0:256], packed[...]) + dot(fwd[:, 256:512], packed[...])

    def tile(step, carry):
        rows = pl.ds(pl.multiple_of(step * 8, 8), 8)
        below = pl.ds(pl.multiple_of(step * 8 + 128, 8), 8)
        values = []
        for i in range(8):
            lanes = slice(128 * i, 128 * i + 128)
            value = (spec[rows, lanes], spec[below, lanes])
            other = (pltpu.roll(value[0], 64, 1), pltpu.roll(value[1], 64, 1))
            a = cmul(value, (twist[0, rows, lanes], twist[1, rows, lanes]))
            b = cmul(other, (twist[2, rows, lanes], twist[3, rows, lanes]))
            values.append((a[0] + b[0], a[1] + b[1]))
        for k, value in enumerate(fft(values, -1)):
            re, im = cmul(value, (factors[0, k, rows, :], factors[1, k, rows, :]))
            filtered[0, k, rows, :] = re
            filtered[1, k, rows, :] = im
        return carry

    lax.fori_loop(0, 16, tile, 0)

    for kappa in range(16):
        block = jnp.concatenate(
            [filtered[ri, k, pl.ds(kappa, 8, stride=16), :] for ri in range(2) for k in range(8)], axis=0
        )
        high, low = halves(block.T)
        both = dot(high, bwd[0]) + dot(low, bwd[0]) + dot(high, bwd[1])
        summed = both[0:64, 0:256] + both[64:128, 256:512]
        re, im = cmul(
            (summed[:, 0:128], summed[:, 128:256]),
            (last[0, kappa : kappa + 1, :], last[1, kappa : kappa + 1, :]),
        )
        parts[0, kappa] = re
        parts[1, kappa] = im

    def rows_out(step, carry):
        rows = pl.ds(pl.multiple_of(step * 16, 16), 16)
        values = [(parts[0, kappa, rows, :], parts[1, kappa, rows, :]) for kappa in range(16)]
        for alpha, (re, im) in enumerate(fft(values, 1)):
            lanes = slice(128 * alpha, 128 * alpha + 128)
            out[0, rows, lanes] = re.astype(BF16)
            out[1, rows, lanes] = im.astype(BF16)
        return carry

    lax.fori_loop(0, 4, rows_out, 0)


def focus_columns(lines, factors):
    fwd, twist, bwd, last = azimuth_tables()
    return pl.pallas_call(
        focus_kernel,
        out_shape=jax.ShapeDtypeStruct((2, ROWS, A), BF16),
        in_specs=[VMEM] * 6,
        out_specs=VMEM,
        scratch_shapes=[
            pltpu.VMEM((2048, 128), F32),
            pltpu.VMEM((256, 1024), BF16),
            pltpu.VMEM((256, 1024), F32),
            pltpu.VMEM((2, 8, 128, 128), F32),
            pltpu.VMEM((2, 16, ROWS, 128), F32),
        ],
        compiler_params=pltpu.CompilerParams(vmem_limit_bytes=VMEM_BYTES),
        cost_estimate=pl.CostEstimate(flops=10**9, bytes_accessed=4 * 10**6, transcendentals=0),
        name="focus_columns",
    )(lines, factors, fwd, twist, bwd, last)


def window_rows(pooled, row_count):
    return sum(pooled[pl.ds(j, row_count // 4, stride=4), :] for j in range(4))


def old_kernel(archive, pooling, out, pooled):
    for date in range(2):
        total = jnp.zeros((ROWS, 128), F32)
        for chunk in range(8):
            lanes = slice(256 * chunk, 256 * chunk + 256)
            re, im = archive[date, 0, :, lanes].astype(F32), archive[date, 1, :, lanes].astype(F32)
            high, low = halves(re * re + im * im)
            total += dot(high, pooling[lanes, :]) + dot(low, pooling[lanes, :])
        pooled[ROWS * date : ROWS * date + ROWS, :] = total
    scale = lax.rsqrt(window_rows(pooled, 2 * ROWS) * (1.0 / 64) + EPSILON)
    out[...] = scale.reshape(2, 16, 128)


def old_scales(archive):
    return pl.pallas_call(
        old_kernel,
        out_shape=jax.ShapeDtypeStruct((2, 128, 128), F32),
        grid=(8,),
        in_specs=[pl.BlockSpec((2, 2, ROWS, A), lambda g: (0, 0, g, 0)), VMEM],
        out_specs=pl.BlockSpec((2, 16, 128), lambda g: (0, g, 0)),
        scratch_shapes=[pltpu.VMEM((2 * ROWS, 128), F32)],
        compiler_params=pltpu.CompilerParams(vmem_limit_bytes=VMEM_BYTES),
        cost_estimate=pl.CostEstimate(flops=10**9, bytes_accessed=9 * 10**6, transcendentals=0),
        name="old_scales",
    )(archive, pooling_table())


def cross_block(image, archives, pooling, pooled):
    total = [jnp.zeros((2 * ROWS, 128), F32) for _ in range(4)]
    power = jnp.zeros((ROWS, 128), F32)
    for chunk in range(8):
        lanes = slice(256 * chunk, 256 * chunk + 256)
        new_re, new_im = image[0, :, lanes].astype(F32), image[1, :, lanes].astype(F32)
        pool = pooling[lanes, :]
        power += dot((new_re * new_re + new_im * new_im).astype(BF16), pool)
        for date in range(4):
            old = archives[date // 2]
            old_re, old_im = old[date % 2, 0, :, lanes].astype(F32), old[date % 2, 1, :, lanes].astype(F32)
            real = new_re * old_re + new_im * old_im
            imag = new_im * old_re - new_re * old_im
            total[date] += dot(jnp.concatenate([real, imag], axis=0).astype(BF16), pool)
    for date in range(4):
        pooled[2 * ROWS * date : 2 * ROWS * (date + 1), :] = total[date]
    pooled[8 * ROWS : 9 * ROWS, :] = power
    sums = window_rows(pooled, 9 * ROWS) * (1.0 / 64)
    scale = lax.rsqrt(sums[128:144] + EPSILON)
    return sums[0:128].reshape(2, 2, 2, 16, 128) * scale


def first_kernel(where, image, own, other, pooling, own_out, other_out, pooled):
    result = cross_block(image, (own, other), pooling, pooled)
    own_out[...] = result[0]
    other_out[...] = result[1]


def rest_kernel(where, image1, image2, image3, own, other, pooling, own_first, other_first, own_out, other_out, pooled):
    step = pl.program_id(0)

    def put(block, own_part, other_part):
        rows = pl.ds(pl.multiple_of(block * 16, 16), 16)
        own_out[:, :, rows, :] = own_part
        other_out[:, :, rows, :] = other_part

    @pl.when(step == 0)
    def _():
        put(where[4], own_first[...], other_first[...])

    for n, image in enumerate((image1, image2, image3)):

        @pl.when(step == n)
        def _(n=n, image=image):
            result = cross_block(image, (own, other), pooling, pooled)
            put(where[5 + n], result[0], result[1])


def archive_spec(offset):
    return pl.BlockSpec((2, 2, ROWS, A), lambda g, where: (0, 0, where[g + offset], 0))


CROSS_PARAMS = dict(compiler_params=pltpu.CompilerParams(vmem_limit_bytes=VMEM_BYTES))


def cross_first(where, image, own, other):
    part = jax.ShapeDtypeStruct((2, 2, 16, 128), F32)
    return pl.pallas_call(
        first_kernel,
        out_shape=(part, part),
        grid_spec=pltpu.PrefetchScalarGridSpec(
            num_scalar_prefetch=1,
            grid=(1,),
            in_specs=[VMEM, archive_spec(0), archive_spec(0), VMEM],
            out_specs=(VMEM, VMEM),
            scratch_shapes=[pltpu.VMEM((9 * ROWS, 128), F32)],
        ),
        cost_estimate=pl.CostEstimate(flops=10**9, bytes_accessed=3 * 10**6, transcendentals=0),
        name="cross_first",
        **CROSS_PARAMS,
    )(where, image, own, other, pooling_table())


def cross_rest(where, images, own, other, first):
    whole = jax.ShapeDtypeStruct((2, 2, 64, 128), F32)
    return pl.pallas_call(
        rest_kernel,
        out_shape=(whole, whole),
        grid_spec=pltpu.PrefetchScalarGridSpec(
            num_scalar_prefetch=1,
            grid=(3,),
            in_specs=[VMEM] * 3 + [archive_spec(1), archive_spec(1)] + [VMEM] * 3,
            out_specs=(VMEM, VMEM),
            scratch_shapes=[pltpu.VMEM((9 * ROWS, 128), F32)],
        ),
        cost_estimate=pl.CostEstimate(flops=3 * 10**9, bytes_accessed=9 * 10**6, transcendentals=0),
        name="cross_rest",
        **CROSS_PARAMS,
    )(where, *images, own, other, pooling_table(), *first)


def final_kernel(where, order, mine, received, scales, out):
    core, first_slot = where[8], where[9]
    for rows, source in ((core, mine), (1 - core, received)):
        rows = pl.ds(pl.multiple_of(rows * 64, 64), 64)
        for n in range(2):
            slot = order[n] - first_slot
            out[n, :, rows, :] = source[slot] * scales[slot, rows, :]


def assemble(where, date_order, mine, received, scales):
    return pl.pallas_call(
        final_kernel,
        out_shape=jax.ShapeDtypeStruct((2, 2, 128, 128), F32),
        in_specs=[pl.BlockSpec(memory_space=pltpu.SMEM)] * 2 + [VMEM] * 3,
        out_specs=VMEM,
        cost_estimate=pl.CostEstimate(flops=10**6, bytes_accessed=10**6, transcendentals=0),
        name="assemble",
    )(where, date_order, mine, received, scales)


def pairs(step):
    out = []
    for date in range(16):
        zh, y, core = step(date // 8, date // 2 % 4, date % 2)
        out.append((date, zh * 8 + y % 4 * 2 + core))
    return out


OTHER_CORE = pairs(lambda zh, y, core: (zh, y, 1 - core))
OTHER_Z = pairs(lambda zh, y, core: (1 - zh, y, core))
NEXT_Y = pairs(lambda zh, y, core: (zh, y + 1, core))
LAST_Y = pairs(lambda zh, y, core: (zh, y + 3, core))


def on_device(raw_echoes, range_phase, azimuth_phase, archive, date_order):
    date = lax.axis_index("date")
    zh, y, core = date // 8, date // 2 % 4, date % 2
    block = (y + 2 * zh) % 4
    blocks = jnp.stack([block, (block + 2) % 4, (block + 3) % 4, (block + 1) % 4])
    where = jnp.concatenate([core * 4 + blocks, blocks, jnp.stack([core, date * 2])]).astype(jnp.int32)

    messages = compress_range(raw_echoes, range_phase)
    messages, azimuth_phase, archive = lax.optimization_barrier((messages, azimuth_phase, archive))
    lines = lax.all_to_all(messages, ALL, 0, 0, tiled=True)
    other_archive = lax.ppermute(archive, "date", OTHER_CORE)
    factors = phase_factors(azimuth_phase, where)
    scales = old_scales(archive)
    image = focus_columns(lines, factors)
    images = [lax.ppermute(image, "date", perm) for perm in (OTHER_Z, NEXT_Y, LAST_Y)]
    first = cross_first(where, image, archive, other_archive)
    mine, others = cross_rest(where, images, archive, other_archive, first)
    received = lax.ppermute(others, "date", OTHER_CORE)
    return assemble(where, date_order, mine, received, scales)


def solution(mesh):
    return jax.shard_map(
        on_device,
        mesh=mesh,
        in_specs=(P(None, ALL, None), P(), P("pixel", None), P("date", None, "pixel", None), P("date")),
        out_specs=P("date", None, "pixel", None),
        check_vma=False,
    )
```

profile of v0, /device:TPU:1, one launch (start us, length us, event | category | flops | bytes accessed | tf_op | source)
XLA Modules:
  0.0 74.2 jit_solution(9845514130747888868)
XLA Ops:
  0.0 0.8 %reshape.3 = f32[128,32]{1,0:T(8,128)S(1)} reshape(f32[4096]{0:T(1024)} %param.16) | data formatting | bytes 32768 | tf_op jit(solution)/shard_map/reshape | solution.py:180
  0.8 0.1 copy.16
  0.9 1.0 %copy-done.3 = bf16[256,512]{1,0:T(8,128)(2,1)S(1)} copy-done((bf16[256,512]{1,0:T(8,128)(2,1)S(1)}, bf16[256,512]{1,0:T(8,128)(2,1)}, u32[]{:S(2)}) %copy-start.3) | copy-done | bytes 262168
  1.9 0.9 %copy-done.9 = bf16[2,16,4096]{2,1,0:T(8,128)(2,1)S(1)} copy-done((bf16[2,16,4096]{2,1,0:T(8,128)(2,1)S(1)}, bf16[2,16,4096]{2,1,0:T(8,128)(2,1)}, u32[]{:S(2)}) %copy-start.9) | copy-done | bytes 262168
  2.8 0.9 %copy-done.10 = bf16[256,512]{1,0:T(8,128)(2,1)S(1)} copy-done((bf16[256,512]{1,0:T(8,128)(2,1)S(1)}, bf16[256,512]{1,0:T(8,128)(2,1)}, u32[]{:S(2)}) %copy-start.10) | copy-done | bytes 262168
  3.8 0.8 %copy-done.11 = f32[2,32,128]{2,1,0:T(8,128)S(1)} copy-done((f32[2,32,128]{2,1,0:T(8,128)S(1)}, f32[2,32,128]{2,1,0:T(8,128)}, u32[]{:S(2)}) %copy-start.11) | copy-done | bytes 32792
  4.5 2.2 %compress_range.1 = bf16[128,16,128]{2,1,0:T(8,128)(2,1)} custom-call(bf16[2,16,4096]{2,1,0:T(8,128)(2,1)S(1)} %copy-done.9, f32[32,128]{1,0:T(8,128)S(1)} %bitcast.7, f32[2,32,128]{2,1,0:T(8,128)S(1)} %copy-done.11, bf16[256,512]{1,0:T(8,128)(2,1)S(1)} %copy-done.10, bf16[256,512]{1,0:T(8,128)(2,1)S(1)} %copy-done.3), custom_call_target="tpu_custom_call" | custom-call | flops 400000000 | bytes 2000000 | tf_op jit(solution)/shard_map/compress_range/pallas_call | solution.py:171
  6.7 1.4 %collective-permute-start.3 = (bf16[2,2,512,2048]{3,2,1,0:T(8,128)(2,1)}, bf16[2,2,512,2048]{3,2,1,0:T(8,128)(2,1)}, u32[]{:S(2)}, u32[]{:S(2)}) collective-permute-start(bf16[2,2,512,2048]{3,2,1,0:T(8,128)(2,1)} %archive), channel_id=1, source_target_pairs={{0,1},{1,0},{2,3},{3,2},{4,5},{5,4},{6,7},{7,6},{8,9},{9,8},{10,11... | collective-permute-start | bytes 25165832 | tf_op jit(solution)/shard_map/ppermute | solution.py:447
  8.1 10.2 %all-to-all-start = ((bf16[128,16,128]{2,1,0:T(8,128)(2,1)}), bf16[128,16,128]{2,1,0:T(8,128)(2,1)S(1)}, u32[]{:S(2)}, u32[]{:S(2)}) async-start(bf16[128,16,128]{2,1,0:T(8,128)(2,1)} %compress_range.1), calls=%async_computation | async-start | bytes 1048576 | tf_op jit(solution)/shard_map/all_to_all | solution.py:446
  18.4 0.1 add_add_fusion
  18.5 0.1 concatenate.4.where
  18.6 1.6 %copy-done.1 = bf16[512,2048]{1,0:T(8,128)(2,1)S(1)} copy-done((bf16[512,2048]{1,0:T(8,128)(2,1)S(1)}, bf16[512,2048]{1,0:T(8,128)(2,1)}, u32[]{:S(2)}) %copy-start.1) | copy-done | bytes 2097176
  20.2 2.5 %phase_factors.1.factors = f32[2,8,128,128]{3,2,1,0:T(8,128)S(1)} custom-call(s32[10]{0:T(128)S(1)} %concatenate.4.where, bf16[512,2048]{1,0:T(8,128)(2,1)S(1)} %copy-done.1), custom_call_target="tpu_custom_call" | custom-call | flops 10000000 | bytes 2000000 | tf_op jit(solution)/shard_map/phase_factors/pallas_call | solution.py:194
  22.7 9.4 %all-to-all-done.lines = bf16[128,16,128]{2,1,0:T(8,128)(2,1)S(1)} async-done(((bf16[128,16,128]{2,1,0:T(8,128)(2,1)}), bf16[128,16,128]{2,1,0:T(8,128)(2,1)S(1)}, u32[]{:S(2)}, u32[]{:S(2)}) %all-to-all-start) | async-done | bytes 524320 | tf_op jit(solution)/shard_map/all_to_all | solution.py:446
  32.1 0.9 %copy-done.4 = bf16[256,512]{1,0:T(8,128)(2,1)S(1)} copy-done((bf16[256,512]{1,0:T(8,128)(2,1)S(1)}, bf16[256,512]{1,0:T(8,128)(2,1)}, u32[]{:S(2)}) %copy-start.4) | copy-done | bytes 262168
  33.1 0.9 %copy-done.5 = bf16[2,128,512]{2,1,0:T(8,128)(2,1)S(1)} copy-done((bf16[2,128,512]{2,1,0:T(8,128)(2,1)S(1)}, bf16[2,128,512]{2,1,0:T(8,128)(2,1)}, u32[]{:S(2)}) %copy-start.5) | copy-done | bytes 262168
  34.0 0.7 copy-done.7
  34.7 6.2 %focus_columns.1.image = bf16[2,64,2048]{2,1,0:T(8,128)(2,1)S(1)} custom-call(bf16[128,16,128]{2,1,0:T(8,128)(2,1)S(1)} %all-to-all-done.lines, f32[2,8,128,128]{3,2,1,0:T(8,128)S(1)} %phase_factors.1.factors, bf16[256,512]{1,0:T(8,128)(2,1)S(1)} %copy-done.4, f32[4,128,1024]{2,1,0:T(8,128)} %constant.84.clone.twist, bf16[2,128,512]{2,1,0:T(8,128)(2,1)S(1)} %copy-done.5, ...), custom_call_target="tpu_custom_call" | custom-call | flops 1000000000 | bytes 4000000 | tf_op jit(solution)/shard_map/focus_columns/pallas_call | solution.py:263
  40.9 0.8 %collective-permute-start = (bf16[2,64,2048]{2,1,0:T(8,128)(2,1)S(1)}, bf16[2,64,2048]{2,1,0:T(8,128)(2,1)S(1)}, u32[]{:S(2)}, u32[]{:S(2)}) collective-permute-start(bf16[2,64,2048]{2,1,0:T(8,128)(2,1)S(1)} %focus_columns.1.image), channel_id=1, source_target_pairs={{0,8},{1,9},{2,10},{3,11},{4,12},{5,13},{6,14},{7,15},{8,0},{9,1},... | collective-permute-start | bytes 1572872 | tf_op jit(solution)/shard_map/ppermute | solution.py:451
  41.8 0.0 collective-permute-start.1
  41.8 2.7 %collective-permute-start.2 = (bf16[2,64,2048]{2,1,0:T(8,128)(2,1)S(1)}, bf16[2,64,2048]{2,1,0:T(8,128)(2,1)S(1)}, u32[]{:S(2)}, u32[]{:S(2)}) collective-permute-start(bf16[2,64,2048]{2,1,0:T(8,128)(2,1)S(1)} %focus_columns.1.image), channel_id=1, source_target_pairs={{0,6},{1,7},{2,0},{3,1},{4,2},{5,3},{6,4},{7,5},{8,14},{9,15},{10,... | collective-permute-start | bytes 1572872 | tf_op jit(solution)/shard_map/ppermute | solution.py:451
  44.5 3.3 %cross_first.1 = (f32[2,2,16,128]{3,2,1,0:T(8,128)S(1)}, f32[2,2,16,128]{3,2,1,0:T(8,128)S(1)}) custom-call(s32[10]{0:T(128)S(1)} %concatenate.4.where, bf16[2,64,2048]{2,1,0:T(8,128)(2,1)S(1)} %focus_columns.1.image, bf16[2,2,512,2048]{3,2,1,0:T(8,128)(2,1)} %archive, bf16[2,2,512,2048]{3,2,1,0:T(8,128)(2,1)} %collective-permute-done.3.other, ...), custom_call_target="tpu_custom_call" | custom-call | flops 1000000000 | bytes 3000000 | tf_op jit(solution)/shard_map/cross_first/pallas_call | solution.py:369
  47.7 7.9 %collective-permute-done.image1 = bf16[2,64,2048]{2,1,0:T(8,128)(2,1)S(1)} collective-permute-done((bf16[2,64,2048]{2,1,0:T(8,128)(2,1)S(1)}, bf16[2,64,2048]{2,1,0:T(8,128)(2,1)S(1)}, u32[]{:S(2)}, u32[]{:S(2)}) %collective-permute-start) | collective-permute-done | bytes 524320 | tf_op jit(solution)/shard_map/ppermute | solution.py:451
  55.6 0.0 collective-permute-done.1.image2
  55.6 0.0 collective-permute-done.2.image3
  55.6 6.0 %cross_rest.1 = (f32[2,2,64,128]{3,2,1,0:T(8,128)S(1)}, f32[2,2,64,128]{3,2,1,0:T(8,128)S(1)}) custom-call(s32[10]{0:T(128)S(1)} %concatenate.4.where, bf16[2,64,2048]{2,1,0:T(8,128)(2,1)S(1)} %collective-permute-done.image1, bf16[2,64,2048]{2,1,0:T(8,128)(2,1)S(1)} %collective-permute-done.1.image2, bf16[2,64,2048]{2,1,0:T(8,128)(2,1)S(1)} %collective-permute-done.2.image3, ...), custom_call_target="tpu_custom_call" | custom-call | flops 3000000000 | bytes 9000000 | tf_op jit(solution)/shard_map/cross_rest/pallas_call | solution.py:387
  61.6 1.8 %collective-permute-start.4 = (f32[2,2,64,128]{3,2,1,0:T(8,128)S(1)}, f32[2,2,64,128]{3,2,1,0:T(8,128)S(1)}, u32[]{:S(2)}, u32[]{:S(2)}) collective-permute-start(f32[2,2,64,128]{3,2,1,0:T(8,128)S(1)} %get-tuple-element.18), channel_id=1, source_target_pairs={{0,1},{1,0},{2,3},{3,2},{4,5},{5,4},{6,7},{7,6},{8,9},{9,8},{10,11... | collective-permute-start | bytes 393224 | tf_op jit(solution)/shard_map/ppermute | solution.py:454
  63.5 7.7 %old_scales.1.scales = f32[2,128,128]{2,1,0:T(8,128)S(1)} custom-call(bf16[2,2,512,2048]{3,2,1,0:T(8,128)(2,1)} %archive, bf16[2048,128]{1,0:T(8,128)(2,1)S(1)} %copy-done), custom_call_target="tpu_custom_call" | custom-call | flops 1000000000 | bytes 9000000 | tf_op jit(solution)/shard_map/old_scales/pallas_call | solution.py:299
  71.2 0.6 copy-done.2
  71.8 0.0 collective-permute-done.4.received
  71.8 0.6 copy-done.12
  72.5 1.8 %assemble.1 = f32[2,2,128,128]{3,2,1,0:T(8,128)} custom-call(s32[10]{0:T(128)} %copy-done.8, s32[2]{0:T(128)} %order.1, f32[2,2,64,128]{3,2,1,0:T(8,128)} %copy-done.6, f32[2,2,64,128]{3,2,1,0:T(8,128)} %copy-done.12, f32[2,128,128]{2,1,0:T(8,128)} %copy-done.2), custom_call_target="tpu_custom_call" | custom-call | flops 1000000 | bytes 1000000 | tf_op jit(solution)/shard_map/assemble/pallas_call | solution.py:413
  (17 shorter events, 0.0 us)
Async XLA Ops:
  0.0 44.5 %copy-start = (bf16[2048,128]{1,0:T(8,128)(2,1)S(1)}, bf16[2048,128]{1,0:T(8,128)(2,1)}, u32[]{:S(2)}) copy-start(bf16[2048,128]{1,0:T(8,128)(2,1)} %constant.83.clone.pooling) | copy-start | bytes 1572868
  0.9 1.0 %copy-start.3 = (bf16[256,512]{1,0:T(8,128)(2,1)S(1)}, bf16[256,512]{1,0:T(8,128)(2,1)}, u32[]{:S(2)}) copy-start(bf16[256,512]{1,0:T(8,128)(2,1)} %constant.82.clone.bwd.fwd) | copy-start | bytes 786436
  1.9 0.9 %copy-start.9 = (bf16[2,16,4096]{2,1,0:T(8,128)(2,1)S(1)}, bf16[2,16,4096]{2,1,0:T(8,128)(2,1)}, u32[]{:S(2)}) copy-start(bf16[2,16,4096]{2,1,0:T(8,128)(2,1)} %raw.1) | copy-start | bytes 786436
  2.8 0.9 %copy-start.10 = (bf16[256,512]{1,0:T(8,128)(2,1)S(1)}, bf16[256,512]{1,0:T(8,128)(2,1)}, u32[]{:S(2)}) copy-start(bf16[256,512]{1,0:T(8,128)(2,1)} %constant.81.clone.fwd) | copy-start | bytes 786436
  3.8 0.8 %copy-start.11 = (f32[2,32,128]{2,1,0:T(8,128)S(1)}, f32[2,32,128]{2,1,0:T(8,128)}, u32[]{:S(2)}) copy-start(f32[2,32,128]{2,1,0:T(8,128)} %constant.80.clone.twist) | copy-start | bytes 98308
  6.7 37.7 %collective-permute-start.3 = (bf16[2,2,512,2048]{3,2,1,0:T(8,128)(2,1)}, bf16[2,2,512,2048]{3,2,1,0:T(8,128)(2,1)}, u32[]{:S(2)}, u32[]{:S(2)}) collective-permute-start(bf16[2,2,512,2048]{3,2,1,0:T(8,128)(2,1)} %archive), channel_id=1, source_target_pairs={{0,1},{1,0},{2,3},{3,2},{4,5},{5,4},{6,7},{7,6},{8,9},{9,8},{10,11... | collective-permute-start | bytes 25165832 | tf_op jit(solution)/shard_map/ppermute | solution.py:447
  8.1 24.0 %all-to-all-start = ((bf16[128,16,128]{2,1,0:T(8,128)(2,1)}), bf16[128,16,128]{2,1,0:T(8,128)(2,1)S(1)}, u32[]{:S(2)}, u32[]{:S(2)}) async-start(bf16[128,16,128]{2,1,0:T(8,128)(2,1)} %compress_range.1), calls=%async_computation | async-start | bytes 1048576 | tf_op jit(solution)/shard_map/all_to_all | solution.py:446
  18.6 1.6 %copy-start.1 = (bf16[512,2048]{1,0:T(8,128)(2,1)S(1)}, bf16[512,2048]{1,0:T(8,128)(2,1)}, u32[]{:S(2)}) copy-start(bf16[512,2048]{1,0:T(8,128)(2,1)} %angle) | copy-start | bytes 6291460
  20.2 35.4 %copy-start.8 = (s32[10]{0:T(128)}, s32[10]{0:T(128)S(1)}, u32[]{:S(2)}) copy-start(s32[10]{0:T(128)S(1)} %concatenate.4.where) | copy-start | bytes 124
  32.1 1.0 %copy-start.4 = (bf16[256,512]{1,0:T(8,128)(2,1)S(1)}, bf16[256,512]{1,0:T(8,128)(2,1)}, u32[]{:S(2)}) copy-start(bf16[256,512]{1,0:T(8,128)(2,1)} %constant.82.clone.bwd.fwd) | copy-start | bytes 786436
  33.1 0.9 %copy-start.5 = (bf16[2,128,512]{2,1,0:T(8,128)(2,1)S(1)}, bf16[2,128,512]{2,1,0:T(8,128)(2,1)}, u32[]{:S(2)}) copy-start(bf16[2,128,512]{2,1,0:T(8,128)(2,1)} %constant.85.clone.bwd) | copy-start | bytes 786436
  34.0 0.7 copy-start.7
  40.9 14.6 %collective-permute-start = (bf16[2,64,2048]{2,1,0:T(8,128)(2,1)S(1)}, bf16[2,64,2048]{2,1,0:T(8,128)(2,1)S(1)}, u32[]{:S(2)}, u32[]{:S(2)}) collective-permute-start(bf16[2,64,2048]{2,1,0:T(8,128)(2,1)S(1)} %focus_columns.1.image), channel_id=1, source_target_pairs={{0,8},{1,9},{2,10},{3,11},{4,12},{5,13},{6,14},{7,15},{8,0},{9,1},... | collective-permute-start | bytes 1572872 | tf_op jit(solution)/shard_map/ppermute | solution.py:451
  41.8 13.8 %collective-permute-start.1 = (bf16[2,64,2048]{2,1,0:T(8,128)(2,1)S(1)}, bf16[2,64,2048]{2,1,0:T(8,128)(2,1)S(1)}, u32[]{:S(2)}, u32[]{:S(2)}) collective-permute-start(bf16[2,64,2048]{2,1,0:T(8,128)(2,1)S(1)} %focus_columns.1.image), channel_id=1, source_target_pairs={{0,2},{1,3},{2,4},{3,5},{4,6},{5,7},{6,0},{7,1},{8,10},{9,11},{10,... | collective-permute-start | bytes 1572872 | tf_op jit(solution)/shard_map/ppermute | solution.py:451
  41.8 13.8 %collective-permute-start.2 = (bf16[2,64,2048]{2,1,0:T(8,128)(2,1)S(1)}, bf16[2,64,2048]{2,1,0:T(8,128)(2,1)S(1)}, u32[]{:S(2)}, u32[]{:S(2)}) collective-permute-start(bf16[2,64,2048]{2,1,0:T(8,128)(2,1)S(1)} %focus_columns.1.image), channel_id=1, source_target_pairs={{0,6},{1,7},{2,0},{3,1},{4,2},{5,3},{6,4},{7,5},{8,14},{9,15},{10,... | collective-permute-start | bytes 1572872 | tf_op jit(solution)/shard_map/ppermute | solution.py:451
  61.6 9.5 %copy-start.6 = (f32[2,2,64,128]{3,2,1,0:T(8,128)}, f32[2,2,64,128]{3,2,1,0:T(8,128)S(1)}, u32[]{:S(2)}) copy-start(f32[2,2,64,128]{3,2,1,0:T(8,128)S(1)} %get-tuple-element.17.mine) | copy-start | bytes 393220
  61.6 10.2 %collective-permute-start.4 = (f32[2,2,64,128]{3,2,1,0:T(8,128)S(1)}, f32[2,2,64,128]{3,2,1,0:T(8,128)S(1)}, u32[]{:S(2)}, u32[]{:S(2)}) collective-permute-start(f32[2,2,64,128]{3,2,1,0:T(8,128)S(1)} %get-tuple-element.18), channel_id=1, source_target_pairs={{0,1},{1,0},{2,3},{3,2},{4,5},{5,4},{6,7},{7,6},{8,9},{9,8},{10,11... | collective-permute-start | bytes 393224 | tf_op jit(solution)/shard_map/ppermute | solution.py:454
  71.2 0.6 copy-start.2
  71.8 0.7 copy-start.12
where the time goes:
time: 75 us; the launch traced here: 74.2 us
  Pallas kernels  29.7 us (40%)
  waiting for transfers between devices  17.2 us (23%)
  starting transfers between devices  16.9 us (23%)
  local copies, waits for them, and re-layouts  10.1 us (13%)
    all_to_all x1, starting transfers between devices, on_device(): lines = lax.all_to_all(messages, ALL, 0, 0, tiled=True)  10.2 us
    all_to_all x1, waiting for transfers between devices, on_device(): lines = lax.all_to_all(messages, ALL, 0, 0, tiled=True)  9.37 us
    unnamed x26, local copies, waits for them, and re-layouts  9.14 us
    ppermute x3, waiting for transfers between devices, on_device(): lax.ppermute(image, 'date', perm)  7.86 us
    pallas_call x1, Pallas kernels, old_scales(): pl.pallas_call(old_kernel, out_shape=jax.ShapeDtypeStruct((2, 128, 128),...  7.69 us
    pallas_call x1, Pallas kernels, focus_columns(): pl.pallas_call(focus_kernel, out_shape=jax.ShapeDtypeStruct((2, ROWS, A),...  6.2 us
    pallas_call x1, Pallas kernels, cross_rest(): pl.pallas_call(rest_kernel, out_shape=(whole, whole), grid_spec=pltpu.Pre...  6.04 us
    ppermute x3, starting transfers between devices, on_device(): lax.ppermute(image, 'date', perm)  3.52 us
  transfers between devices with their start and end apart: 6, of which 2 were waited for; matrix products, arithmetic and copies ran while one was open for 0% of the time, Pallas kernels for 27%

commit v1 on v0

v1 whole, which is shorter than its diff:
```python
import math

import jax
import jax.numpy as jnp
import numpy as np
from jax import lax
from jax.experimental import pallas as pl
from jax.experimental.pallas import tpu as pltpu
from jax.sharding import PartitionSpec as P

F32 = jnp.float32
BF16 = jnp.bfloat16
EPSILON = 1e-06
R = 4096
A = 2048
ROWS = 64
LINES = 16
ALL = ("pixel", "date")
VMEM = pl.BlockSpec(memory_space=pltpu.VMEM)
SMEM = pl.BlockSpec(memory_space=pltpu.SMEM)
HBM = pl.BlockSpec(memory_space=pltpu.HBM)


def cmul(a, b):
    return (a[0] * b[0] - a[1] * b[1], a[0] * b[1] + a[1] * b[0])


def turned(value, k, n, sign):
    if k == 0:
        return value
    re, im = value
    if 8 * k == n:
        return ((re - im) * math.sqrt(0.5), (im + re) * math.sqrt(0.5)) if sign > 0 else (
            (re + im) * math.sqrt(0.5),
            (im - re) * math.sqrt(0.5),
        )
    if 8 * k == 3 * n:
        return ((re + im) * -math.sqrt(0.5), (re - im) * math.sqrt(0.5)) if sign > 0 else (
            (im - re) * math.sqrt(0.5),
            (re + im) * -math.sqrt(0.5),
        )
    angle = sign * 2.0 * math.pi * k / n
    return cmul(value, (math.cos(angle), math.sin(angle)))


def fft(values, sign):
    n = len(values)
    if n == 1:
        return values
    even, odd = fft(values[0::2], sign), fft(values[1::2], sign)
    low, high = [], []
    for k in range(n // 2):
        er, ei = even[k]
        if 4 * k == n:
            tr, ti = odd[k]
            plus, minus = (er - ti, ei + tr), (er + ti, ei - tr)
            low.append(plus if sign > 0 else minus)
            high.append(minus if sign > 0 else plus)
        else:
            tr, ti = turned(odd[k], k, n, sign)
            low.append((er + tr, ei + ti))
            high.append((er - tr, ei - ti))
    return low + high


def split(table):
    table = np.asarray(table, np.float32)
    high = table.astype(BF16)
    low = (table - high.astype(np.float32)).astype(BF16)
    return high, low


def real_form(angle, sign):
    c, s = np.cos(angle), sign * np.sin(angle)
    return np.block([[c, s], [-s, c]])


def range_tables():
    t = np.arange(128)
    k1 = 4 * (t % 32) + t // 32
    angle = 2 * np.pi * np.outer(t, k1) / 128
    fwd = np.concatenate(split(real_form(angle, -1)), axis=1)
    bwd = np.concatenate(split(real_form(angle.T, 1)), axis=1)
    twist = 2 * np.pi * np.outer(np.arange(32), t) / R
    return np.stack([np.cos(twist), -np.sin(twist)]).astype(np.float32), fwd, bwd


def azimuth_tables():
    s = np.arange(128)
    fwd = np.concatenate(split(real_form(2 * np.pi * np.outer(s, s) / 128, -1).T), axis=1)
    k1 = np.arange(128)[:, None]
    i = np.arange(8)[None, :]
    twist = np.stack([np.exp(-2j * np.pi * (i + 8 * half) * k1 / A) for half in (0, 1)], axis=-1)
    twist = np.repeat(np.stack([twist.real, twist.imag]), 64, axis=-1).transpose(0, 2, 1, 3).astype(np.float32)
    odd = np.exp(-2j * np.pi * np.arange(8)[:, None] / 16 * (np.arange(128)[None, :] // 64))
    k, lam = np.meshgrid(np.arange(8), np.arange(8), indexing="ij")
    m = (lam + 16 * k).reshape(64)
    beta = np.arange(128)
    parts = [real_form(2 * np.pi * np.outer(m + 8 * par, beta) / 128, 1) for par in (0, 1)]
    bwd = np.concatenate(split(np.concatenate(parts, axis=0)), axis=1)
    last = 2 * np.pi * np.outer(np.arange(16), beta) / A
    rows = np.concatenate([np.exp(1j * last), odd], axis=0)
    rows = np.stack([rows.real, rows.imag]).astype(np.float32)
    return twist, np.concatenate([fwd, bwd], axis=0), rows


def pooling_table():
    return (np.arange(A)[:, None] // 16 == np.arange(128)[None, :]).astype(BF16)


def dot(a, b):
    return jnp.dot(a, b, preferred_element_type=F32)


def halves(x):
    high = x.astype(BF16)
    return high, (x - high.astype(F32)).astype(BF16)


def dot_split(x, table):
    high, low = halves(x)
    n = table.shape[1] // 2
    return dot(high, table[:, :n]) + dot(low, table[:, :n]) + dot(high, table[:, n:])


def params(mib):
    return pltpu.CompilerParams(vmem_limit_bytes=mib * 2**20)


def cost(flops, moved, transcendentals=0):
    return pl.CostEstimate(flops=flops, bytes_accessed=moved, transcendentals=transcendentals)


def in_hbm(*arrays):
    return [pltpu.with_memory_space_constraint(x, pltpu.HBM) for x in arrays]


def in_vmem(*arrays):
    return [pltpu.with_memory_space_constraint(x, pltpu.VMEM) for x in arrays]


def fetch(sources, targets, sems):
    copies = [
        pltpu.make_async_copy(source, target, sems.at[n]) for n, (source, target) in enumerate(zip(sources, targets))
    ]
    for copy in copies:
        copy.start()
    return copies


def range_kernel(raw_hbm, phase_hbm, twist_hbm, fwd_hbm, bwd_hbm, out, raw, phase, twist, fwd, bwd, a, b, sems):
    copies = fetch(
        (phase_hbm, raw_hbm, twist_hbm, fwd_hbm, bwd_hbm), (phase, raw, twist, fwd, bwd), sems
    )
    copies[0].wait()
    angle = phase[...]
    angle = jnp.concatenate(
        [angle] + [pltpu.roll(angle, 128 - 32 * g, 1) for g in range(1, 4)], axis=0
    ).T[0:32]
    cosine, sine = jnp.cos(angle) * (1.0 / R), jnp.sin(angle) * (1.0 / R)
    copies[1].wait()
    copies[2].wait()
    values = [
        (raw[0, :, 128 * q : 128 * q + 128].astype(F32), raw[1, :, 128 * q : 128 * q + 128].astype(F32))
        for q in range(32)
    ]
    for k0, value in enumerate(fft(values, -1)):
        re, im = cmul(value, (twist[0, k0 : k0 + 1, :], twist[1, k0 : k0 + 1, :]))
        a[16 * k0 : 16 * k0 + 16, 0:128] = re
        a[16 * k0 : 16 * k0 + 16, 128:256] = im
    copies[3].wait()
    b[...] = dot_split(a[...], fwd)
    for k0 in range(32):
        rows = slice(16 * k0, 16 * k0 + 16)
        re, im = cmul((b[rows, 0:128], b[rows, 128:256]), (cosine[k0 : k0 + 1], sine[k0 : k0 + 1]))
        a[rows, 0:128] = re
        a[rows, 128:256] = im
    copies[4].wait()
    b[...] = dot_split(a[...], bwd)
    values = []
    for k0 in range(32):
        rows = slice(16 * k0, 16 * k0 + 16)
        values.append(
            cmul((b[rows, 0:128], b[rows, 128:256]), (twist[0, k0 : k0 + 1, :], -twist[1, k0 : k0 + 1, :]))
        )
    left = lax.broadcasted_iota(jnp.int32, (8, 128), 1) < 64
    for q, value in enumerate(fft(values, 1)):
        for half in range(2):
            parts = []
            for part in value:
                low, high = part[0:8], part[8:16]
                if half == 0:
                    parts.append(jnp.where(left, low, pltpu.roll(high, 64, 1)))
                else:
                    parts.append(jnp.where(left, pltpu.roll(low, 64, 1), high))
            message = jnp.concatenate(parts, axis=0).astype(BF16)
            pixel, core, block = q // 4, (q // 2) % 2, 2 * (q % 2) + half
            for zh in range(2):
                y = (block + 2 * zh) % 4
                out[pixel * 16 + zh * 8 + y * 2 + core] = message


def compress_range(raw, phase):
    twist, fwd, bwd = range_tables()
    return pl.pallas_call(
        range_kernel,
        out_shape=jax.ShapeDtypeStruct((128, 16, 128), BF16),
        in_specs=[HBM] * 5,
        out_specs=VMEM,
        scratch_shapes=[
            pltpu.VMEM((2, 16, R), BF16),
            pltpu.VMEM((32, 128), F32),
            pltpu.VMEM((2, 32, 128), F32),
            pltpu.VMEM((256, 512), BF16),
            pltpu.VMEM((256, 512), BF16),
            pltpu.VMEM((512, 256), F32),
            pltpu.VMEM((512, 256), F32),
            pltpu.SemaphoreType.DMA((5,)),
        ],
        compiler_params=params(24),
        cost_estimate=cost(4 * 10**8, 2 * 10**6, 8192),
        name="compress_range",
    )(*in_hbm(raw, phase.reshape(32, 128), *map(jnp.asarray, (twist, fwd, bwd))))


def prepare_kernel(
    where, angle_hbm, twist_hbm, mats_hbm, last_hbm, factors, mats, last, angle, sems
):
    rows = pl.ds(pl.multiple_of(where[0] * ROWS, ROWS), ROWS)
    copies = fetch(
        (angle_hbm.at[rows], twist_hbm, mats_hbm, last_hbm),
        (angle, factors.at[2:4], mats, last),
        sems,
    )
    copies[0].wait()
    for k in range(8):
        block = jnp.concatenate(
            [angle[:, 256 * k : 256 * k + 128], angle[:, 256 * k + 128 : 256 * k + 256]], axis=0
        )
        turned_block = block.astype(F32).T
        factors[0, k] = jnp.cos(turned_block) * (1.0 / A)
        factors[1, k] = jnp.sin(turned_block) * (1.0 / A)
    for copy in copies[1:]:
        copy.wait()


def prepare(azimuth_phase, where):
    tables = azimuth_tables()
    return pl.pallas_call(
        prepare_kernel,
        out_shape=(pltpu.VMEM((4, 8, 128, 128), F32), *(pltpu.VMEM(t.shape, t.dtype) for t in tables[1:])),
        in_specs=[SMEM] + [HBM] * 4,
        out_specs=(VMEM,) * 3,
        scratch_shapes=[pltpu.VMEM((ROWS, A), BF16), pltpu.SemaphoreType.DMA((4,))],
        compiler_params=params(24),
        cost_estimate=cost(10**7, 8 * 10**6, 262144),
        name="prepare",
    )(where, *in_hbm(azimuth_phase, *map(jnp.asarray, tables)))


def focus_kernel(lines, factors, mats, last, out, wide, packed, spec, filtered, turned_rows, parts):
    wide[...] = lines[...].reshape(2048, 128).astype(F32)
    for j in range(16):
        ri, i = j // 8, j % 8
        packed[128 * ri : 128 * ri + 128, 128 * i : 128 * i + 128] = wide[pl.ds(j, 128, stride=16), :].astype(BF16)
    spec[...] = dot(mats[0:256, 0:256], packed[...]) + dot(mats[0:256, 256:512], packed[...])

    sign = jnp.where(lax.broadcasted_iota(jnp.int32, (8, 128), 1) < 64, 1.0, -1.0)

    def tile(step, carry):
        rows = pl.ds(pl.multiple_of(step * 8, 8), 8)
        below = pl.ds(pl.multiple_of(step * 8 + 128, 8), 8)
        values = []
        for i in range(8):
            lanes = slice(128 * i, 128 * i + 128)
            value = cmul((spec[rows, lanes], spec[below, lanes]), (factors[2, i, rows, :], factors[3, i, rows, :]))
            value = tuple(pltpu.roll(part, 64, 1) + part * sign for part in value)
            if i:
                value = cmul(value, (last[0, 16 + i : 17 + i, :], last[1, 16 + i : 17 + i, :]))
            values.append(value)
        for k, value in enumerate(fft(values, -1)):
            re, im = cmul(value, (factors[0, k, rows, :], factors[1, k, rows, :]))
            filtered[0, k, rows, :] = re
            filtered[1, k, rows, :] = im
        return carry

    lax.fori_loop(0, 16, tile, 0, unroll=4)

    for kappa in range(16):
        block = jnp.concatenate(
            [filtered[ri, k, pl.ds(kappa, 8, stride=16), :] for ri in range(2) for k in range(8)], axis=0
        )
        block = block.T.astype(BF16)
        turned_rows[64 * kappa : 64 * kappa + 64, 0:128] = block[0:64]
        turned_rows[64 * kappa : 64 * kappa + 64, 128:256] = block[64:128]
    parts[...] = dot(turned_rows[...], mats[256:512, 0:256]) + dot(turned_rows[...], mats[256:512, 256:512])

    def rows_out(step, carry):
        rows = pl.ds(pl.multiple_of(step * 16, 16), 16)
        values = []
        for kappa in range(16):
            here = pl.ds(pl.multiple_of(step * 16 + 64 * kappa, 16), 16)
            values.append(
                cmul(
                    (parts[here, 0:128], parts[here, 128:256]),
                    (last[0, kappa : kappa + 1, :], last[1, kappa : kappa + 1, :]),
                )
            )
        for alpha, (re, im) in enumerate(fft(values, 1)):
            lanes = slice(128 * alpha, 128 * alpha + 128)
            out[0, rows, lanes] = re.astype(BF16)
            out[1, rows, lanes] = im.astype(BF16)
        return carry

    lax.fori_loop(0, 4, rows_out, 0, unroll=2)


def focus_columns(lines, factors, mats, last):
    return pl.pallas_call(
        focus_kernel,
        out_shape=jax.ShapeDtypeStruct((2, ROWS, A), BF16),
        in_specs=[VMEM] * 4,
        out_specs=VMEM,
        scratch_shapes=[
            pltpu.VMEM((2048, 128), F32),
            pltpu.VMEM((256, 1024), BF16),
            pltpu.VMEM((256, 1024), F32),
            pltpu.VMEM((2, 8, 128, 128), F32),
            pltpu.VMEM((1024, 256), BF16),
            pltpu.VMEM((1024, 256), F32),
        ],
        compiler_params=params(24),
        cost_estimate=cost(10**9, 4 * 10**6),
        name="focus_columns",
    )(lines, factors, mats, last)


def window_rows(pooled, row_count):
    return sum(pooled[pl.ds(j, row_count // 4, stride=4), :] for j in range(4)) * (1.0 / 64)


def old_kernel(archive, pooling, out, products, pooled):
    for date in range(2):
        for chunk in range(8):
            lanes = slice(256 * chunk, 256 * chunk + 256)
            re, im = archive[date, 0, :, lanes], archive[date, 1, :, lanes]
            products[ROWS * date : ROWS * date + ROWS, lanes] = re * re + im * im
    pooled[...] = dot(products[...], pooling[...])
    out[...] = lax.rsqrt(window_rows(pooled, 2 * ROWS) + EPSILON).reshape(2, 16, 128)


def old_scales(archive, pooling):
    return pl.pallas_call(
        old_kernel,
        out_shape=jax.ShapeDtypeStruct((2, 128, 128), F32),
        grid=(8,),
        in_specs=[
            pl.BlockSpec((2, 2, ROWS, A), lambda g: (0, 0, g, 0)),
            pl.BlockSpec((A, 128), lambda g: (0, 0)),
        ],
        out_specs=pl.BlockSpec((2, 16, 128), lambda g: (0, g, 0)),
        scratch_shapes=[pltpu.VMEM((2 * ROWS, A), BF16), pltpu.VMEM((2 * ROWS, 128), F32)],
        compiler_params=params(24),
        cost_estimate=cost(10**9, 9 * 10**6),
        name="old_scales",
    )(*in_hbm(archive, pooling))


def cross_products(products, row, image, old, old_rows):
    for chunk in range(8):
        lanes = slice(256 * chunk, 256 * chunk + 256)
        new_re, new_im = image[0, :, lanes], image[1, :, lanes]
        old_re, old_im = old[0, old_rows, lanes], old[1, old_rows, lanes]
        products[row : row + ROWS, lanes] = new_re * old_re + new_im * old_im
        products[row + ROWS : row + 2 * ROWS, lanes] = new_im * old_re - new_re * old_im


def power_products(products, row, image):
    for chunk in range(8):
        lanes = slice(256 * chunk, 256 * chunk + 256)
        new_re, new_im = image[0, :, lanes], image[1, :, lanes]
        products[row : row + ROWS, lanes] = new_re * new_re + new_im * new_im


ALL_ROWS = slice(0, ROWS)


def first_kernel(
    where, image, own, other, pooling_hbm, own_out, other_out, held, pooling, here, products, pooled, sems
):
    copies = []
    for n in range(4):
        rows = pl.ds(pl.multiple_of(where[n] * ROWS, ROWS), ROWS)
        for m, source in enumerate((own, other)):
            if n == 0:
                target = here.at[2 * m : 2 * m + 2]
            else:
                target = held.at[2 * m : 2 * m + 2, :, ROWS * (n - 1) : ROWS * n]
            copies.append(pltpu.make_async_copy(source.at[:, :, rows], target, sems.at[2 * n + m]))
            copies[-1].start()
    copies.insert(2, pltpu.make_async_copy(pooling_hbm, pooling, sems.at[8]))
    copies[2].start()
    power_products(products, 8 * ROWS, image)
    copies[0].wait()
    copies[1].wait()
    for date in range(4):
        cross_products(products, 2 * ROWS * date, image, here.at[date], ALL_ROWS)
    copies[2].wait()
    pooled[...] = dot(products[...], pooling[...])
    sums = window_rows(pooled, 9 * ROWS)
    result = sums[0:128].reshape(2, 2, 2, 16, 128) * lax.rsqrt(sums[128:144] + EPSILON)
    own_out[...] = result[0]
    other_out[...] = result[1]
    for copy in copies[3:]:
        copy.wait()


def cross_first(where, image, own, other, pooling):
    part = jax.ShapeDtypeStruct((2, 2, 16, 128), F32)
    return pl.pallas_call(
        first_kernel,
        out_shape=(part, part, pltpu.VMEM((4, 2, 3 * ROWS, A), BF16), pltpu.VMEM((A, 128), BF16)),
        in_specs=[SMEM, VMEM, HBM, HBM, HBM],
        out_specs=(VMEM,) * 4,
        scratch_shapes=[
            pltpu.VMEM((4, 2, ROWS, A), BF16),
            pltpu.VMEM((9 * ROWS, A), BF16),
            pltpu.VMEM((9 * ROWS, 128), F32),
            pltpu.SemaphoreType.DMA((9,)),
        ],
        compiler_params=params(24),
        cost_estimate=cost(10**9, 8 * 10**6),
        name="cross_first",
    )(where, image, *in_hbm(own, other, pooling))


def put(where, n, target, part):
    target[:, :, pl.ds(pl.multiple_of(where[4 + n] * 16, 16), 16), :] = part


def other_kernel(where, image1, image2, image3, held, pooling, first, out, new_scale, products, pooled):
    images = (image1, image2, image3)
    for n, image in enumerate(images):
        power_products(products, 12 * ROWS + ROWS * n, image)
        for date in range(2):
            cross_products(
                products, 2 * ROWS * (2 * n + date), image, held.at[2 + date], slice(ROWS * n, ROWS * n + ROWS)
            )
    pooled[...] = dot(products[...], pooling[...])
    sums = window_rows(pooled, 15 * ROWS)
    scale = lax.rsqrt(sums[192:240] + EPSILON)
    new_scale[...] = scale
    put(where, 0, out, first[...])
    for n in range(3):
        part = sums[64 * n : 64 * n + 64].reshape(2, 2, 16, 128)
        put(where, n + 1, out, part * scale[16 * n : 16 * n + 16])


def cross_others(where, images, held, pooling, first):
    return pl.pallas_call(
        other_kernel,
        out_shape=(jax.ShapeDtypeStruct((2, 2, 64, 128), F32), jax.ShapeDtypeStruct((48, 128), F32)),
        in_specs=[SMEM] + [VMEM] * 6,
        out_specs=(VMEM, VMEM),
        scratch_shapes=[pltpu.VMEM((15 * ROWS, A), BF16), pltpu.VMEM((15 * ROWS, 128), F32)],
        compiler_params=params(24),
        cost_estimate=cost(10**9, 9 * 10**6),
        name="cross_others",
    )(where, *images, held, pooling, first)


def own_kernel(where, order, image1, image2, image3, held, pooling, first, new_scale, scales, out, products, pooled, total):
    for n, image in enumerate((image1, image2, image3)):
        for date in range(2):
            cross_products(products, 2 * ROWS * (2 * n + date), image, held.at[date], slice(ROWS * n, ROWS * n + ROWS))
    pooled[...] = dot(products[...], pooling[...])
    sums = window_rows(pooled, 12 * ROWS)
    put(where, 0, total, first[...])
    for n in range(3):
        part = sums[64 * n : 64 * n + 64].reshape(2, 2, 16, 128)
        put(where, n + 1, total, part * new_scale[16 * n : 16 * n + 16])
    rows = pl.ds(pl.multiple_of(where[8] * 64, 64), 64)
    for n in range(2):
        slot = order[n] - where[9]
        out[n, :, rows, :] = total[slot] * scales[slot, rows, :]


def cross_own(where, order, images, held, pooling, first, new_scale, scales):
    return pl.pallas_call(
        own_kernel,
        out_shape=jax.ShapeDtypeStruct((2, 2, 128, 128), F32),
        in_specs=[SMEM] * 2 + [VMEM] * 8,
        out_specs=VMEM,
        scratch_shapes=[
            pltpu.VMEM((12 * ROWS, A), BF16),
            pltpu.VMEM((12 * ROWS, 128), F32),
            pltpu.VMEM((2, 2, 64, 128), F32),
        ],
        compiler_params=params(24),
        cost_estimate=cost(10**9, 9 * 10**6),
        name="cross_own",
    )(where, order, *images, held, pooling, first, new_scale, scales)


def final_kernel(where, order, half, received, scales, out):
    rows = pl.ds(pl.multiple_of(where[8] * 64, 64), 64)
    out[:, :, rows, :] = half[:, :, rows, :]
    rows = pl.ds(pl.multiple_of((1 - where[8]) * 64, 64), 64)
    for n in range(2):
        slot = order[n] - where[9]
        out[n, :, rows, :] = received[slot] * scales[slot, rows, :]


def assemble(where, order, half, received, scales):
    return pl.pallas_call(
        final_kernel,
        out_shape=jax.ShapeDtypeStruct((2, 2, 128, 128), F32),
        in_specs=[SMEM] * 2 + [VMEM] * 3,
        out_specs=VMEM,
        compiler_params=params(24),
        cost_estimate=cost(10**6, 10**6),
        name="assemble",
    )(where, order, half, received, scales)


def pairs(step):
    out = []
    for date in range(16):
        zh, y, core = step(date // 8, date // 2 % 4, date % 2)
        out.append((date, zh * 8 + y % 4 * 2 + core))
    return out


OTHER_CORE = pairs(lambda zh, y, core: (zh, y, 1 - core))
OTHER_Z = pairs(lambda zh, y, core: (1 - zh, y, core))
NEXT_Y = pairs(lambda zh, y, core: (zh, y + 1, core))
LAST_Y = pairs(lambda zh, y, core: (zh, y + 3, core))


def on_device(raw_echoes, range_phase, azimuth_phase, archive, date_order):
    date = lax.axis_index("date")
    zh, y, core = date // 8, date // 2 % 4, date % 2
    block = (y + 2 * zh) % 4
    blocks = jnp.stack([block, (block + 2) % 4, (block + 3) % 4, (block + 1) % 4])
    where = jnp.concatenate([core * 4 + blocks, blocks, jnp.stack([core, date * 2])]).astype(jnp.int32)

    messages = compress_range(raw_echoes, range_phase)
    messages, azimuth_phase, archive = lax.optimization_barrier((messages, azimuth_phase, archive))
    lines = lax.all_to_all(messages, ALL, 0, 0, tiled=True)
    other_archive = lax.ppermute(archive, "date", OTHER_CORE)
    image = focus_columns(lines, *prepare(azimuth_phase, where))
    pooling = jnp.asarray(pooling_table())
    images = [lax.ppermute(image, "date", perm) for perm in (OTHER_Z, NEXT_Y, LAST_Y)]
    scales = old_scales(archive, pooling)
    own_first, other_first, held, pooling = cross_first(where, image, archive, other_archive, pooling)
    other_first, scales = lax.optimization_barrier((other_first, scales))
    others, new_scale = cross_others(where, images, held, pooling, other_first)
    received = lax.ppermute(others, "date", OTHER_CORE)
    half = cross_own(where, date_order, images, held, pooling, own_first, new_scale, scales)
    return assemble(where, date_order, half, received, scales)


def solution(mesh):
    return jax.shard_map(
        on_device,
        mesh=mesh,
        in_specs=(P(None, ALL, None), P(), P("pixel", None), P("date", None, "pixel", None), P("date")),
        out_specs=P("date", None, "pixel", None),
        check_vma=False,
    )
```

time: 75 us -> 54.1 us (0.72)
  local copies, waits for them, and re-layouts: 10.1 us -> 0.09 us
  waiting for transfers between devices: 17.2 us -> 9.98 us
  Pallas kernels: 29.7 us -> 26 us
    unnamed x26 -> x2, local copies, waits for them, and re-layouts: 9.14 us -> 0.01 us
    ppermute x3, waiting for transfers between devices: 7.86 us -> 0.01 us  [on_device(): lax.ppermute(image, 'date', perm)]
    pallas_call x1, Pallas kernels: 6.2 us -> 2.6 us  [focus_columns(): pl.pallas_call(focus_kernel, out_shape=jax.ShapeDtypeStruct((2, ROWS, A),...]
    pallas_call x1, Pallas kernels: 2.16 us -> 3.39 us  [compress_range(): pl.pallas_call(range_kernel, out_shape=jax.ShapeDtypeStruct((128, 16, 128...]
    reshape x2 -> x0, local copies, waits for them, and re-layouts: 0.91 us -> none  [compress_range(): phase.reshape(128, 32)]
    pallas_call x1, Pallas kernels: 7.69 us -> 6.89 us  [old_scales(): pl.pallas_call(old_kernel, out_shape=jax.ShapeDtypeStruct((2, 128, 128),...]
    pallas_call x3 -> x4, Pallas kernels: 11.8 us -> 11.9 us  [the longest x1 4.95 us: cross_first(): pl.pallas_call(first_kernel, out_shape=(part, part, pltpu.VMEM((4, 2, 3 *...]
  transfers between devices with their start and end apart: 6 -> 6, of which waited for: 2 -> 1; matrix products, arithmetic and copies ran while one was open for 0% -> 0% of each run, Pallas kernels for 27% -> 36%
where the time goes in v1:
time: 54.1 us; the launch traced here: 53.7 us
  Pallas kernels  26 us (48%)
  starting transfers between devices  17.3 us (32%)
  waiting for transfers between devices  9.98 us (18%)
    all_to_all x1, starting transfers between devices, on_device(): lines = lax.all_to_all(messages, ALL, 0, 0, tiled=True)  10.2 us
    all_to_all x1, waiting for transfers between devices, on_device(): lines = lax.all_to_all(messages, ALL, 0, 0, tiled=True)  9.97 us
    pallas_call x1, Pallas kernels, old_scales(): pl.pallas_call(old_kernel, out_shape=jax.ShapeDtypeStruct((2, 128, 128),...  6.89 us
    pallas_call x1, Pallas kernels, cross_first(): pl.pallas_call(first_kernel, out_shape=(part, part, pltpu.VMEM((4, 2, 3 *...  4.95 us
    pallas_call x1, Pallas kernels, prepare(): pl.pallas_call(prepare_kernel, out_shape=(pltpu.VMEM((4, 8, 128, 128), F3...  3.53 us
    ppermute x3, starting transfers between devices, on_device(): lax.ppermute(image, 'date', perm)  3.52 us
    pallas_call x1, Pallas kernels, compress_range(): pl.pallas_call(range_kernel, out_shape=jax.ShapeDtypeStruct((128, 16, 128...  3.39 us
    pallas_call x1, Pallas kernels, focus_columns(): pl.pallas_call(focus_kernel, out_shape=jax.ShapeDtypeStruct((2, ROWS, A),...  2.6 us
  transfers between devices with their start and end apart: 6, of which 1 were waited for; matrix products, arithmetic and copies ran while one was open for 0% of the time, Pallas kernels for 36%

profile of v1, /device:TPU:1, one launch (start us, length us, event | category | flops | bytes accessed | tf_op | source)
XLA Modules:
  0.0 53.7 jit_solution(12922286944681795255)
XLA Ops:
  0.0 3.4 %compress_range.1 = bf16[128,16,128]{2,1,0:T(8,128)(2,1)} custom-call(bf16[2,16,4096]{2,1,0:T(8,128)(2,1)} %raw_hbm.1, f32[32,128]{1,0:T(8,128)} %bitcast.7, f32[2,32,128]{2,1,0:T(8,128)} %constant.80.clone.twist_hbm, bf16[256,512]{1,0:T(8,128)(2,1)} %constant.81.clone.fwd_hbm, bf16[256,512]{1,0:T(8,128)(2,1)} %constant.82.clone.bwd_hbm), custom_call_target="tpu_custom_call" | custom-call | flops 400000000 | bytes 2000000 | tf_op jit(solution)/shard_map/compress_range/pallas_call | solution.py:205
  3.4 1.5 %collective-permute-start.3 = (bf16[2,2,512,2048]{3,2,1,0:T(8,128)(2,1)}, bf16[2,2,512,2048]{3,2,1,0:T(8,128)(2,1)}, u32[]{:S(2)}, u32[]{:S(2)}) collective-permute-start(bf16[2,2,512,2048]{3,2,1,0:T(8,128)(2,1)} %archive), channel_id=1, source_target_pairs={{0,1},{1,0},{2,3},{3,2},{4,5},{5,4},{6,7},{7,6},{8,9},{9,8},{10,11... | collective-permute-start | bytes 25165832 | tf_op jit(solution)/shard_map/ppermute | solution.py:550
  4.9 10.2 %all-to-all-start = ((bf16[128,16,128]{2,1,0:T(8,128)(2,1)}), bf16[128,16,128]{2,1,0:T(8,128)(2,1)S(1)}, u32[]{:S(2)}, u32[]{:S(2)}) async-start(bf16[128,16,128]{2,1,0:T(8,128)(2,1)} %compress_range.1), calls=%async_computation | async-start | bytes 1048576 | tf_op jit(solution)/shard_map/all_to_all | solution.py:549
  15.2 0.1 add_add_fusion
  15.3 0.1 concatenate.4.where
  15.4 3.5 %prepare.1 = (f32[4,8,128,128]{3,2,1,0:T(8,128)S(1)}, bf16[512,512]{1,0:T(8,128)(2,1)S(1)}, f32[2,24,128]{2,1,0:T(8,128)S(1)}) custom-call(s32[10]{0:T(128)S(1)} %concatenate.4.where, bf16[512,2048]{1,0:T(8,128)(2,1)} %angle_hbm, f32[2,8,128,128]{3,2,1,0:T(8,128)} %constant.83.clone.twist_hbm, bf16[512,512]{1,0:T(8,128)(2,1)} %constant.84.clone.mats_hbm, ...), custom_call_target="tpu_custom_call" | custom-call | flops 10000000 | bytes 8000000 | tf_op jit(solution)/shard_map/prepare/pallas_call | solution.py:249
  18.9 10.0 %all-to-all-done.lines = bf16[128,16,128]{2,1,0:T(8,128)(2,1)S(1)} async-done(((bf16[128,16,128]{2,1,0:T(8,128)(2,1)}), bf16[128,16,128]{2,1,0:T(8,128)(2,1)S(1)}, u32[]{:S(2)}, u32[]{:S(2)}) %all-to-all-start) | async-done | bytes 524320 | tf_op jit(solution)/shard_map/all_to_all | solution.py:549
  28.9 2.6 %focus_columns.1.image = bf16[2,64,2048]{2,1,0:T(8,128)(2,1)S(1)} custom-call(bf16[128,16,128]{2,1,0:T(8,128)(2,1)S(1)} %all-to-all-done.lines, f32[4,8,128,128]{3,2,1,0:T(8,128)S(1)} %get-tuple-element.21.factors, bf16[512,512]{1,0:T(8,128)(2,1)S(1)} %get-tuple-element.22.mats, f32[2,24,128]{2,1,0:T(8,128)S(1)} %get-tuple-element.23.last), custom_call_target="tpu_custom_call" | custom-call | flops 1000000000 | bytes 4000000 | tf_op jit(solution)/shard_map/focus_columns/pallas_call | solution.py:319
  31.5 0.8 %collective-permute-start = (bf16[2,64,2048]{2,1,0:T(8,128)(2,1)S(1)}, bf16[2,64,2048]{2,1,0:T(8,128)(2,1)S(1)}, u32[]{:S(2)}, u32[]{:S(2)}) collective-permute-start(bf16[2,64,2048]{2,1,0:T(8,128)(2,1)S(1)} %focus_columns.1.image), channel_id=1, source_target_pairs={{0,8},{1,9},{2,10},{3,11},{4,12},{5,13},{6,14},{7,15},{8,0},{9,1},... | collective-permute-start | bytes 1572872 | tf_op jit(solution)/shard_map/ppermute | solution.py:553
  32.3 0.0 collective-permute-start.1
  32.3 2.7 %collective-permute-start.2 = (bf16[2,64,2048]{2,1,0:T(8,128)(2,1)S(1)}, bf16[2,64,2048]{2,1,0:T(8,128)(2,1)S(1)}, u32[]{:S(2)}, u32[]{:S(2)}) collective-permute-start(bf16[2,64,2048]{2,1,0:T(8,128)(2,1)S(1)} %focus_columns.1.image), channel_id=1, source_target_pairs={{0,6},{1,7},{2,0},{3,1},{4,2},{5,3},{6,4},{7,5},{8,14},{9,15},{10,... | collective-permute-start | bytes 1572872 | tf_op jit(solution)/shard_map/ppermute | solution.py:553
  35.0 6.9 %old_scales.1.scales = f32[2,128,128]{2,1,0:T(8,128)S(1)} custom-call(bf16[2,2,512,2048]{3,2,1,0:T(8,128)(2,1)} %archive, bf16[2048,128]{1,0:T(8,128)(2,1)} %constant.86.clone.pooling_hbm.pooling), custom_call_target="tpu_custom_call" | custom-call | flops 1000000000 | bytes 9000000 | tf_op jit(solution)/shard_map/old_scales/pallas_call | solution.py:353
  41.9 0.0 collective-permute-done.3.other
  41.9 4.9 %cross_first.1 = (f32[2,2,16,128]{3,2,1,0:T(8,128)S(1)}, f32[2,2,16,128]{3,2,1,0:T(8,128)S(1)}, bf16[4,2,192,2048]{3,2,1,0:T(8,128)(2,1)S(1)}, bf16[2048,128]{1,0:T(8,128)(2,1)S(1)}) custom-call(s32[10]{0:T(128)S(1)} %concatenate.4.where, bf16[2,64,2048]{2,1,0:T(8,128)(2,1)S(1)} %focus_columns.1.image, bf16[2,2,512,2048]{3,2,1,0:T(8,128)(2,1)} %archive, ...), custom_call_target="tpu_custom_call" | custom-call | flops 1000000000 | bytes 8000000 | tf_op jit(solution)/shard_map/cross_first/pallas_call | solution.py:420
  46.9 0.0 copy-start
  46.9 0.0 collective-permute-done.image1
  46.9 0.0 collective-permute-done.1.image2
  46.9 0.0 collective-permute-done.2.image3
  46.9 1.8 %cross_others.1 = (f32[2,2,64,128]{3,2,1,0:T(8,128)S(1)}, f32[48,128]{1,0:T(8,128)S(1)}) custom-call(s32[10]{0:T(128)S(1)} %concatenate.4.where, bf16[2,64,2048]{2,1,0:T(8,128)(2,1)S(1)} %collective-permute-done.image1, bf16[2,64,2048]{2,1,0:T(8,128)(2,1)S(1)} %collective-permute-done.1.image2, bf16[2,64,2048]{2,1,0:T(8,128)(2,1)S(1)} %collective-permute-done.2.image3, ...), custom_call_target="tpu_custom_call" | custom-call | flops 1000000000 | bytes 9000000 | tf_op jit(solution)/shard_map/cross_others/pallas_call | solution.py:460
  48.7 2.1 %collective-permute-start.4 = (f32[2,2,64,128]{3,2,1,0:T(8,128)S(1)}, f32[2,2,64,128]{3,2,1,0:T(8,128)S(1)}, u32[]{:S(2)}, u32[]{:S(2)}) collective-permute-start(f32[2,2,64,128]{3,2,1,0:T(8,128)S(1)} %get-tuple-element.32), channel_id=1, source_target_pairs={{0,1},{1,0},{2,3},{3,2},{4,5},{5,4},{6,7},{7,6},{8,9},{9,8},{10,11... | collective-permute-start | bytes 393224 | tf_op jit(solution)/shard_map/ppermute | solution.py:558
  50.8 0.0 copy-done
  50.8 1.6 %cross_own.1.half = f32[2,2,128,128]{3,2,1,0:T(8,128)S(1)} custom-call(s32[10]{0:T(128)S(1)} %concatenate.4.where, s32[2]{0:T(128)S(1)} %copy-done, bf16[2,64,2048]{2,1,0:T(8,128)(2,1)S(1)} %collective-permute-done.image1, bf16[2,64,2048]{2,1,0:T(8,128)(2,1)S(1)} %collective-permute-done.1.image2, bf16[2,64,2048]{2,1,0:T(8,128)(2,1)S(1)} %collective-permute-done.2.image3, ...), custom_call_target="tpu_custom_call" | custom-call | flops 1000000000 | bytes 9000000 | tf_op jit(solution)/shard_map/cross_own/pallas_call | solution.py:489
  52.5 0.0 collective-permute-done.4.received
  52.5 1.3 %assemble.1 = f32[2,2,128,128]{3,2,1,0:T(8,128)} custom-call(s32[10]{0:T(128)S(1)} %concatenate.4.where, s32[2]{0:T(128)S(1)} %copy-done, f32[2,2,128,128]{3,2,1,0:T(8,128)S(1)} %cross_own.1.half, f32[2,2,64,128]{3,2,1,0:T(8,128)S(1)} %collective-permute-done.4.received, f32[2,128,128]{2,1,0:T(8,128)S(1)} %old_scales.1.scales), custom_call_target="tpu_custom_call" | custom-call | flops 1000000 | bytes 1000000 | tf_op jit(solution)/shard_map/assemble/pallas_call | solution.py:515
Async XLA Ops:
  3.4 38.5 %collective-permute-start.3 = (bf16[2,2,512,2048]{3,2,1,0:T(8,128)(2,1)}, bf16[2,2,512,2048]{3,2,1,0:T(8,128)(2,1)}, u32[]{:S(2)}, u32[]{:S(2)}) collective-permute-start(bf16[2,2,512,2048]{3,2,1,0:T(8,128)(2,1)} %archive), channel_id=1, source_target_pairs={{0,1},{1,0},{2,3},{3,2},{4,5},{5,4},{6,7},{7,6},{8,9},{9,8},{10,11... | collective-permute-start | bytes 25165832 | tf_op jit(solution)/shard_map/ppermute | solution.py:550
  4.9 24.0 %all-to-all-start = ((bf16[128,16,128]{2,1,0:T(8,128)(2,1)}), bf16[128,16,128]{2,1,0:T(8,128)(2,1)S(1)}, u32[]{:S(2)}, u32[]{:S(2)}) async-start(bf16[128,16,128]{2,1,0:T(8,128)(2,1)} %compress_range.1), calls=%async_computation | async-start | bytes 1048576 | tf_op jit(solution)/shard_map/all_to_all | solution.py:549
  31.5 15.4 %collective-permute-start = (bf16[2,64,2048]{2,1,0:T(8,128)(2,1)S(1)}, bf16[2,64,2048]{2,1,0:T(8,128)(2,1)S(1)}, u32[]{:S(2)}, u32[]{:S(2)}) collective-permute-start(bf16[2,64,2048]{2,1,0:T(8,128)(2,1)S(1)} %focus_columns.1.image), channel_id=1, source_target_pairs={{0,8},{1,9},{2,10},{3,11},{4,12},{5,13},{6,14},{7,15},{8,0},{9,1},... | collective-permute-start | bytes 1572872 | tf_op jit(solution)/shard_map/ppermute | solution.py:553
  32.3 14.6 %collective-permute-start.1 = (bf16[2,64,2048]{2,1,0:T(8,128)(2,1)S(1)}, bf16[2,64,2048]{2,1,0:T(8,128)(2,1)S(1)}, u32[]{:S(2)}, u32[]{:S(2)}) collective-permute-start(bf16[2,64,2048]{2,1,0:T(8,128)(2,1)S(1)} %focus_columns.1.image), channel_id=1, source_target_pairs={{0,2},{1,3},{2,4},{3,5},{4,6},{5,7},{6,0},{7,1},{8,10},{9,11},{10,... | collective-permute-start | bytes 1572872 | tf_op jit(solution)/shard_map/ppermute | solution.py:553
  32.3 14.6 %collective-permute-start.2 = (bf16[2,64,2048]{2,1,0:T(8,128)(2,1)S(1)}, bf16[2,64,2048]{2,1,0:T(8,128)(2,1)S(1)}, u32[]{:S(2)}, u32[]{:S(2)}) collective-permute-start(bf16[2,64,2048]{2,1,0:T(8,128)(2,1)S(1)} %focus_columns.1.image), channel_id=1, source_target_pairs={{0,6},{1,7},{2,0},{3,1},{4,2},{5,3},{6,4},{7,5},{8,14},{9,15},{10,... | collective-permute-start | bytes 1572872 | tf_op jit(solution)/shard_map/ppermute | solution.py:553
  46.9 4.0 %copy-start = (s32[2]{0:T(128)S(1)}, s32[2]{0:T(128)}, u32[]{:S(2)}) copy-start(s32[2]{0:T(128)} %order.3) | copy-start | bytes 28
  48.7 3.8 %collective-permute-start.4 = (f32[2,2,64,128]{3,2,1,0:T(8,128)S(1)}, f32[2,2,64,128]{3,2,1,0:T(8,128)S(1)}, u32[]{:S(2)}, u32[]{:S(2)}) collective-permute-start(f32[2,2,64,128]{3,2,1,0:T(8,128)S(1)} %get-tuple-element.32), channel_id=1, source_target_pairs={{0,1},{1,0},{2,3},{3,2},{4,5},{5,4},{6,7},{7,6},{8,9},{9,8},{10,11... | collective-permute-start | bytes 393224 | tf_op jit(solution)/shard_map/ppermute | solution.py:558

commit v2 on v1

--- a/solution.py
+++ b/solution.py
@@ -1,3 +1,4 @@
+from functools import partial
 import math
 
 import jax
@@ -17,7 +18,6 @@
 LINES = 16
 ALL = ("pixel", "date")
 VMEM = pl.BlockSpec(memory_space=pltpu.VMEM)
-SMEM = pl.BlockSpec(memory_space=pltpu.SMEM)
 HBM = pl.BlockSpec(memory_space=pltpu.HBM)
 
 
@@ -146,6 +146,18 @@
     for copy in copies:
         copy.start()
     return copies
+
+
+def place():
+    date = lax.axis_index("date")
+    zh, y, core = lax.shift_right_logical(date, 3), lax.shift_right_logical(date, 1) & 3, date & 1
+    block = (y + 2 * zh) & 3
+    return core, (block, (block + 2) & 3, (block + 3) & 3, (block + 1) & 3)
+
+
+def archive_rows(n):
+    core, blocks = place()
+    return pl.ds(pl.multiple_of((4 * core + blocks[n]) * ROWS, ROWS), ROWS)
 
 
 def range_kernel(raw_hbm, phase_hbm, twist_hbm, fwd_hbm, bwd_hbm, out, raw, phase, twist, fwd, bwd, a, b, sems):
@@ -223,10 +235,8 @@
     )(*in_hbm(raw, phase.reshape(32, 128), *map(jnp.asarray, (twist, fwd, bwd))))
 
 
-def prepare_kernel(
-    where, angle_hbm, twist_hbm, mats_hbm, last_hbm, factors, mats, last, angle, sems
-):
-    rows = pl.ds(pl.multiple_of(where[0] * ROWS, ROWS), ROWS)
+def prepare_kernel(angle_hbm, twist_hbm, mats_hbm, last_hbm, factors, mats, last, angle, sems):
+    rows = archive_rows(0)
     copies = fetch(
         (angle_hbm.at[rows], twist_hbm, mats_hbm, last_hbm),
         (angle, factors.at[2:4], mats, last),
@@ -244,18 +254,18 @@
         copy.wait()
 
 
-def prepare(azimuth_phase, where):
+def prepare(azimuth_phase):
     tables = azimuth_tables()
     return pl.pallas_call(
         prepare_kernel,
         out_shape=(pltpu.VMEM((4, 8, 128, 128), F32), *(pltpu.VMEM(t.shape, t.dtype) for t in tables[1:])),
-        in_specs=[SMEM] + [HBM] * 4,
+        in_specs=[HBM] * 4,
         out_specs=(VMEM,) * 3,
         scratch_shapes=[pltpu.VMEM((ROWS, A), BF16), pltpu.SemaphoreType.DMA((4,))],
         compiler_params=params(24),
         cost_estimate=cost(10**7, 8 * 10**6, 262144),
         name="prepare",
-    )(where, *in_hbm(azimuth_phase, *map(jnp.asarray, tables)))
+    )(*in_hbm(azimuth_phase, *map(jnp.asarray, tables)))
 
 
 def focus_kernel(lines, factors, mats, last, out, wide, packed, spec, filtered, turned_rows, parts):
@@ -290,16 +300,19 @@
         block = jnp.concatenate(
             [filtered[ri, k, pl.ds(kappa, 8, stride=16), :] for ri in range(2) for k in range(8)], axis=0
         )
-        block = block.T.astype(BF16)
-        turned_rows[64 * kappa : 64 * kappa + 64, 0:128] = block[0:64]
-        turned_rows[64 * kappa : 64 * kappa + 64, 128:256] = block[64:128]
-    parts[...] = dot(turned_rows[...], mats[256:512, 0:256]) + dot(turned_rows[...], mats[256:512, 256:512])
-
-    def rows_out(step, carry):
-        rows = pl.ds(pl.multiple_of(step * 16, 16), 16)
+        for n, part in enumerate(halves(block.T)):
+            turned_rows[64 * kappa : 64 * kappa + 64, 256 * n : 256 * n + 128] = part[0:64]
+            turned_rows[64 * kappa : 64 * kappa + 64, 256 * n + 128 : 256 * n + 256] = part[64:128]
+    bwd_high, bwd_low = mats[256:512, 0:256], mats[256:512, 256:512]
+    parts[...] = (
+        dot(turned_rows[:, 0:256], bwd_high) + dot(turned_rows[:, 256:512], bwd_high) + dot(turned_rows[:, 0:256], bwd_low)
+    )
+
+    for step in range(4):
+        rows = slice(16 * step, 16 * step + 16)
         values = []
         for kappa in range(16):
-            here = pl.ds(pl.multiple_of(step * 16 + 64 * kappa, 16), 16)
+            here = slice(16 * step + 64 * kappa, 16 * step + 64 * kappa + 16)
             values.append(
                 cmul(
                     (parts[here, 0:128], parts[here, 128:256]),
@@ -310,9 +323,6 @@
             lanes = slice(128 * alpha, 128 * alpha + 128)
             out[0, rows, lanes] = re.astype(BF16)
             out[1, rows, lanes] = im.astype(BF16)
-        return carry
-
-    lax.fori_loop(0, 4, rows_out, 0, unroll=2)
 
 
 def focus_columns(lines, factors, mats, last):
@@ -326,7 +336,7 @@
             pltpu.VMEM((256, 1024), BF16),
             pltpu.VMEM((256, 1024), F32),
             pltpu.VMEM((2, 8, 128, 128), F32),
-            pltpu.VMEM((1024, 256), BF16),
+            pltpu.VMEM((1024, 512), BF16),
             pltpu.VMEM((1024, 256), F32),
         ],
         compiler_params=params(24),
@@ -339,188 +349,194 @@
     return sum(pooled[pl.ds(j, row_count // 4, stride=4), :] for j in range(4)) * (1.0 / 64)
 
 
-def old_kernel(archive, pooling, out, products, pooled):
-    for date in range(2):
-        for chunk in range(8):
-            lanes = slice(256 * chunk, 256 * chunk + 256)
-            re, im = archive[date, 0, :, lanes], archive[date, 1, :, lanes]
-            products[ROWS * date : ROWS * date + ROWS, lanes] = re * re + im * im
-    pooled[...] = dot(products[...], pooling[...])
-    out[...] = lax.rsqrt(window_rows(pooled, 2 * ROWS) + EPSILON).reshape(2, 16, 128)
-
-
-def old_scales(archive, pooling):
-    return pl.pallas_call(
-        old_kernel,
-        out_shape=jax.ShapeDtypeStruct((2, 128, 128), F32),
-        grid=(8,),
-        in_specs=[
-            pl.BlockSpec((2, 2, ROWS, A), lambda g: (0, 0, g, 0)),
-            pl.BlockSpec((A, 128), lambda g: (0, 0)),
-        ],
-        out_specs=pl.BlockSpec((2, 16, 128), lambda g: (0, g, 0)),
-        scratch_shapes=[pltpu.VMEM((2 * ROWS, A), BF16), pltpu.VMEM((2 * ROWS, 128), F32)],
-        compiler_params=params(24),
-        cost_estimate=cost(10**9, 9 * 10**6),
-        name="old_scales",
-    )(*in_hbm(archive, pooling))
+def inverse_root(power):
+    return lax.rsqrt(power + EPSILON)
+
+
+CHUNKS = [slice(256 * n, 256 * n + 256) for n in range(A // 256)]
 
 
 def cross_products(products, row, image, old, old_rows):
-    for chunk in range(8):
-        lanes = slice(256 * chunk, 256 * chunk + 256)
+    for lanes in CHUNKS:
         new_re, new_im = image[0, :, lanes], image[1, :, lanes]
         old_re, old_im = old[0, old_rows, lanes], old[1, old_rows, lanes]
         products[row : row + ROWS, lanes] = new_re * old_re + new_im * old_im
         products[row + ROWS : row + 2 * ROWS, lanes] = new_im * old_re - new_re * old_im
 
 
-def power_products(products, row, image):
-    for chunk in range(8):
-        lanes = slice(256 * chunk, 256 * chunk + 256)
-        new_re, new_im = image[0, :, lanes], image[1, :, lanes]
-        products[row : row + ROWS, lanes] = new_re * new_re + new_im * new_im
+def power_products(products, row, image, rows):
+    for lanes in CHUNKS:
+        re, im = image[0, rows, lanes], image[1, rows, lanes]
+        products[row : row + ROWS, lanes] = re * re + im * im
 
 
 ALL_ROWS = slice(0, ROWS)
 
 
+def block_rows(n):
+    return slice(ROWS * n, ROWS * n + ROWS)
+
+
+def pool(products, pooling, pooled, count):
+    pooled[0 : count * ROWS, :] = dot(products[0 : count * ROWS, :], pooling[...])
+    return window_rows(pooled.at[0 : count * ROWS], count * ROWS).reshape(count, 16, 128)
+
+
+def scratch(count):
+    return [pltpu.VMEM((count * ROWS, A), BF16), pltpu.VMEM((count * ROWS, 128), F32)]
+
+
 def first_kernel(
-    where, image, own, other, pooling_hbm, own_out, other_out, held, pooling, here, products, pooled, sems
+    image, own, other, pooling_hbm, first, held, old_scales, pooling, here, products, pooled, sems
 ):
     copies = []
     for n in range(4):
-        rows = pl.ds(pl.multiple_of(where[n] * ROWS, ROWS), ROWS)
+        rows = archive_rows(n)
         for m, source in enumerate((own, other)):
             if n == 0:
                 target = here.at[2 * m : 2 * m + 2]
             else:
-                target = held.at[2 * m : 2 * m + 2, :, ROWS * (n - 1) : ROWS * n]
+                target = held.at[2 * m : 2 * m + 2, :, block_rows(n - 1)]
             copies.append(pltpu.make_async_copy(source.at[:, :, rows], target, sems.at[2 * n + m]))
             copies[-1].start()
-    copies.insert(2, pltpu.make_async_copy(pooling_hbm, pooling, sems.at[8]))
-    copies[2].start()
-    power_products(products, 8 * ROWS, image)
+    copies.append(pltpu.make_async_copy(pooling_hbm, pooling, sems.at[8]))
+    copies[-1].start()
+    power_products(products, 12 * ROWS, image, ALL_ROWS)
     copies[0].wait()
     copies[1].wait()
     for date in range(4):
-        cross_products(products, 2 * ROWS * date, image, here.at[date], ALL_ROWS)
-    copies[2].wait()
-    pooled[...] = dot(products[...], pooling[...])
-    sums = window_rows(pooled, 9 * ROWS)
-    result = sums[0:128].reshape(2, 2, 2, 16, 128) * lax.rsqrt(sums[128:144] + EPSILON)
-    own_out[...] = result[0]
-    other_out[...] = result[1]
-    for copy in copies[3:]:
-        copy.wait()
-
-
-def cross_first(where, image, own, other, pooling):
-    part = jax.ShapeDtypeStruct((2, 2, 16, 128), F32)
+        cross_products(products, 2 * date * ROWS, image, here.at[date], ALL_ROWS)
+        power_products(products, (8 + date) * ROWS, here.at[date], ALL_ROWS)
+    copies[8].wait()
+    sums = pool(products, pooling, pooled, 13)
+    new = inverse_root(sums[12])
+    for date in range(4):
+        scale = new * inverse_root(sums[8 + date])
+        for part in range(2):
+            first[date, part] = sums[2 * date + part] * scale
+    for n in range(1, 4):
+        copies[2 * n].wait()
+        copies[2 * n + 1].wait()
+        for date in range(4):
+            power_products(products, date * ROWS, held.at[date], block_rows(n - 1))
+        old_scales[n - 1] = inverse_root(pool(products, pooling, pooled, 4))
+
+
+def cross_first(image, own, other, pooling):
     return pl.pallas_call(
         first_kernel,
-        out_shape=(part, part, pltpu.VMEM((4, 2, 3 * ROWS, A), BF16), pltpu.VMEM((A, 128), BF16)),
-        in_specs=[SMEM, VMEM, HBM, HBM, HBM],
+        out_shape=(
+            jax.ShapeDtypeStruct((4, 2, 16, 128), F32),
+            pltpu.VMEM((4, 2, 3 * ROWS, A), BF16),
+            jax.ShapeDtypeStruct((3, 4, 16, 128), F32),
+            pltpu.VMEM((A, 128), BF16),
+        ),
+        in_specs=[VMEM, HBM, HBM, HBM],
         out_specs=(VMEM,) * 4,
-        scratch_shapes=[
-            pltpu.VMEM((4, 2, ROWS, A), BF16),
-            pltpu.VMEM((9 * ROWS, A), BF16),
-            pltpu.VMEM((9 * ROWS, 128), F32),
-            pltpu.SemaphoreType.DMA((9,)),
-        ],
+        scratch_shapes=[pltpu.VMEM((4, 2, ROWS, A), BF16), *scratch(13), pltpu.SemaphoreType.DMA((9,))],
         compiler_params=params(24),
         cost_estimate=cost(10**9, 8 * 10**6),
         name="cross_first",
-    )(where, image, *in_hbm(own, other, pooling))
-
-
-def put(where, n, target, part):
-    target[:, :, pl.ds(pl.multiple_of(where[4 + n] * 16, 16), 16), :] = part
-
-
-def other_kernel(where, image1, image2, image3, held, pooling, first, out, new_scale, products, pooled):
-    images = (image1, image2, image3)
-    for n, image in enumerate(images):
-        power_products(products, 12 * ROWS + ROWS * n, image)
-        for date in range(2):
-            cross_products(
-                products, 2 * ROWS * (2 * n + date), image, held.at[2 + date], slice(ROWS * n, ROWS * n + ROWS)
-            )
-    pooled[...] = dot(products[...], pooling[...])
-    sums = window_rows(pooled, 15 * ROWS)
-    scale = lax.rsqrt(sums[192:240] + EPSILON)
-    new_scale[...] = scale
-    put(where, 0, out, first[...])
-    for n in range(3):
-        part = sums[64 * n : 64 * n + 64].reshape(2, 2, 16, 128)
-        put(where, n + 1, out, part * scale[16 * n : 16 * n + 16])
-
-
-def cross_others(where, images, held, pooling, first):
+    )(image, *in_hbm(own, other, pooling))
+
+
+def block_kernel(n, image, held, old_scales, pooling, out, products, pooled):
+    for date in range(4):
+        cross_products(products, 2 * date * ROWS, image, held.at[date], block_rows(n))
+    power_products(products, 8 * ROWS, image, ALL_ROWS)
+    sums = pool(products, pooling, pooled, 9)
+    new = inverse_root(sums[8])
+    for date in range(4):
+        scale = new * old_scales[n, date]
+        for part in range(2):
+            out[date, part] = sums[2 * date + part] * scale
+
+
+def cross_block(n, image, held, old_scales, pooling):
+    return pl.pallas_call(
+        partial(block_kernel, n),
+        out_shape=jax.ShapeDtypeStruct((4, 2, 16, 128), F32),
+        in_specs=[VMEM] * 4,
+        out_specs=VMEM,
+        scratch_shapes=scratch(9),
+        compiler_params=params(24),
+        cost_estimate=cost(10**8, 4 * 10**6),
+        name="cross_block",
+    )(image, held, old_scales, pooling)
+
+
+def put(n, target, parts):
+    target[:, :, pl.ds(pl.multiple_of(place()[1][n] * 16, 16), 16), :] = parts
+
+
+def other_kernel(image, held, old_scales, pooling, part0, part1, part2, out, new_scale, products, pooled):
+    for date in range(2):
+        cross_products(products, 2 * date * ROWS, image, held.at[2 + date], block_rows(2))
+    power_products(products, 4 * ROWS, image, ALL_ROWS)
+    for n, part in enumerate((part0, part1, part2)):
+        put(n, out, part[2:4])
+    sums = pool(products, pooling, pooled, 5)
+    new = inverse_root(sums[4])
+    new_scale[...] = new
+    put(3, out, sums[0:4].reshape(2, 2, 16, 128) * (new * old_scales[2, 2:4])[:, None])
+
+
+def cross_others(image, held, old_scales, pooling, parts):
     return pl.pallas_call(
         other_kernel,
-        out_shape=(jax.ShapeDtypeStruct((2, 2, 64, 128), F32), jax.ShapeDtypeStruct((48, 128), F32)),
-        in_specs=[SMEM] + [VMEM] * 6,
+        out_shape=(jax.ShapeDtypeStruct((2, 2, 64, 128), F32), jax.ShapeDtypeStruct((16, 128), F32)),
+        in_specs=[VMEM] * 7,
         out_specs=(VMEM, VMEM),
-        scratch_shapes=[pltpu.VMEM((15 * ROWS, A), BF16), pltpu.VMEM((15 * ROWS, 128), F32)],
-        compiler_params=params(24),
-        cost_estimate=cost(10**9, 9 * 10**6),
+        scratch_shapes=scratch(5),
+        compiler_params=params(24),
+        cost_estimate=cost(10**8, 4 * 10**6),
         name="cross_others",
-    )(where, *images, held, pooling, first)
-
-
-def own_kernel(where, order, image1, image2, image3, held, pooling, first, new_scale, scales, out, products, pooled, total):
-    for n, image in enumerate((image1, image2, image3)):
-        for date in range(2):
-            cross_products(products, 2 * ROWS * (2 * n + date), image, held.at[date], slice(ROWS * n, ROWS * n + ROWS))
-    pooled[...] = dot(products[...], pooling[...])
-    sums = window_rows(pooled, 12 * ROWS)
-    put(where, 0, total, first[...])
-    for n in range(3):
-        part = sums[64 * n : 64 * n + 64].reshape(2, 2, 16, 128)
-        put(where, n + 1, total, part * new_scale[16 * n : 16 * n + 16])
-    rows = pl.ds(pl.multiple_of(where[8] * 64, 64), 64)
-    for n in range(2):
-        slot = order[n] - where[9]
-        out[n, :, rows, :] = total[slot] * scales[slot, rows, :]
-
-
-def cross_own(where, order, images, held, pooling, first, new_scale, scales):
+    )(image, held, old_scales, pooling, *parts)
+
+
+def own_kernel(image, held, old_scales, pooling, part0, part1, part2, new_scale, out, products, pooled):
+    for date in range(2):
+        cross_products(products, 2 * date * ROWS, image, held.at[date], block_rows(2))
+    for n, part in enumerate((part0, part1, part2)):
+        put(n, out, part[0:2])
+    sums = pool(products, pooling, pooled, 4)
+    put(3, out, sums.reshape(2, 2, 16, 128) * (new_scale[...] * old_scales[2, 0:2])[:, None])
+
+
+def cross_own(image, held, old_scales, pooling, parts, new_scale):
     return pl.pallas_call(
         own_kernel,
-        out_shape=jax.ShapeDtypeStruct((2, 2, 128, 128), F32),
-        in_specs=[SMEM] * 2 + [VMEM] * 8,
+        out_shape=jax.ShapeDtypeStruct((2, 2, 64, 128), F32),
+        in_specs=[VMEM] * 8,
         out_specs=VMEM,
-        scratch_shapes=[
-            pltpu.VMEM((12 * ROWS, A), BF16),
-            pltpu.VMEM((12 * ROWS, 128), F32),
-            pltpu.VMEM((2, 2, 64, 128), F32),
-        ],
-        compiler_params=params(24),
-        cost_estimate=cost(10**9, 9 * 10**6),
+        scratch_shapes=scratch(4),
+        compiler_params=params(24),
+        cost_estimate=cost(10**8, 4 * 10**6),
         name="cross_own",
-    )(where, order, *images, held, pooling, first, new_scale, scales)
-
-
-def final_kernel(where, order, half, received, scales, out):
-    rows = pl.ds(pl.multiple_of(where[8] * 64, 64), 64)
-    out[:, :, rows, :] = half[:, :, rows, :]
-    rows = pl.ds(pl.multiple_of((1 - where[8]) * 64, 64), 64)
-    for n in range(2):
-        slot = order[n] - where[9]
-        out[n, :, rows, :] = received[slot] * scales[slot, rows, :]
-
-
-def assemble(where, order, half, received, scales):
+    )(image, held, old_scales, pooling, *parts, new_scale)
+
+
+def final_kernel(order, mine, received, out):
+    core, _ = place()
+    odd_first = order[...] & 1 == 1
+    for half, source in ((core, mine), (1 - core, received)):
+        rows = pl.ds(pl.multiple_of(half * 64, 64), 64)
+        for part in range(2):
+            even, odd = source[0, part], source[1, part]
+            out[0, part, rows, :] = jnp.where(odd_first, odd, even)
+            out[1, part, rows, :] = jnp.where(odd_first, even, odd)
+
+
+def assemble(date_order, mine, received):
     return pl.pallas_call(
         final_kernel,
         out_shape=jax.ShapeDtypeStruct((2, 2, 128, 128), F32),
-        in_specs=[SMEM] * 2 + [VMEM] * 3,
+        in_specs=[VMEM] * 3,
         out_specs=VMEM,
         compiler_params=params(24),
         cost_estimate=cost(10**6, 10**6),
         name="assemble",
-    )(where, order, half, received, scales)
+    )(jnp.broadcast_to(date_order[0], (1, 128)), mine, received)
 
 
 def pairs(step):
@@ -538,26 +554,18 @@
 
 
 def on_device(raw_echoes, range_phase, azimuth_phase, archive, date_order):
-    date = lax.axis_index("date")
-    zh, y, core = date // 8, date // 2 % 4, date % 2
-    block = (y + 2 * zh) % 4
-    blocks = jnp.stack([block, (block + 2) % 4, (block + 3) % 4, (block + 1) % 4])
-    where = jnp.concatenate([core * 4 + blocks, blocks, jnp.stack([core, date * 2])]).astype(jnp.int32)
-
     messages = compress_range(raw_echoes, range_phase)
     messages, azimuth_phase, archive = lax.optimization_barrier((messages, azimuth_phase, archive))
     lines = lax.all_to_all(messages, ALL, 0, 0, tiled=True)
     other_archive = lax.ppermute(archive, "date", OTHER_CORE)
-    image = focus_columns(lines, *prepare(azimuth_phase, where))
-    pooling = jnp.asarray(pooling_table())
+    image = focus_columns(lines, *prepare(azimuth_phase))
     images = [lax.ppermute(image, "date", perm) for perm in (OTHER_Z, NEXT_Y, LAST_Y)]
-    scales = old_scales(archive, pooling)
-    own_first, other_first, held, pooling = cross_first(where, image, archive, other_archive, pooling)
-    other_first, scales = lax.optimization_barrier((other_first, scales))
-    others, new_scale = cross_others(where, images, held, pooling, other_first)
+    first, *kept = cross_first(image, archive, other_archive, jnp.asarray(pooling_table()))
+    parts = [first] + [cross_block(n, images[n], *kept) for n in range(2)]
+    others, new_scale = cross_others(images[2], *kept, parts)
     received = lax.ppermute(others, "date", OTHER_CORE)
-    half = cross_own(where, date_order, images, held, pooling, own_first, new_scale, scales)
-    return assemble(where, date_order, half, received, scales)
+    mine = cross_own(images[2], *kept, parts, new_scale)
+    return assemble(date_order, mine, received)
 
 
 def solution(mesh):

time: 54.1 us -> 51.3 us (0.948)
  Pallas kernels: 26 us -> 19.9 us
  waiting for transfers between devices: 9.98 us -> 14.5 us
  starting transfers between devices: 17.3 us -> 16.6 us
    pallas_call x3 -> x4, Pallas kernels: 13.5 us -> 9.74 us  [the longest x1 7.62 us: cross_first(): pl.pallas_call(first_kernel, out_shape=(jax.ShapeDtypeStruct((4, 2, 16, 1...]
    ppermute x3, waiting for transfers between devices: 0.01 us -> 3.2 us  [on_device(): lax.ppermute(image, 'date', perm)]
    pallas_call x1, Pallas kernels: 1.79 us -> 0.54 us  [cross_others(): pl.pallas_call(other_kernel, out_shape=(jax.ShapeDtypeStruct((2, 2, 64, 1...]
    all_to_all x1, waiting for transfers between devices: 9.97 us -> 10.8 us  [on_device(): lines = lax.all_to_all(messages, ALL, 0, 0, tiled=True)]
    ppermute x1, starting transfers between devices: 2.12 us -> 1.36 us  [on_device(): received = lax.ppermute(others, 'date', OTHER_CORE)]
    pallas_call x1, Pallas kernels: 1.27 us -> 0.73 us  [assemble(): pl.pallas_call(final_kernel, out_shape=jax.ShapeDtypeStruct((2, 2, 128, 1...]
  transfers between devices with their start and end apart: 6 -> 6, of which waited for: 1 -> 3; matrix products, arithmetic and copies ran while one was open for 0% -> 0% of each run, Pallas kernels for 36% -> 30%
where the time goes in v2:
time: 51.3 us; the launch traced here: 51.1 us
  Pallas kernels  19.9 us (39%)
  starting transfers between devices  16.6 us (32%)
  waiting for transfers between devices  14.5 us (28%)
    all_to_all x1, waiting for transfers between devices, on_device(): lines = lax.all_to_all(messages, ALL, 0, 0, tiled=True)  10.8 us
    all_to_all x1, starting transfers between devices, on_device(): lines = lax.all_to_all(messages, ALL, 0, 0, tiled=True)  10.2 us
    pallas_call x1, Pallas kernels, cross_first(): pl.pallas_call(first_kernel, out_shape=(jax.ShapeDtypeStruct((4, 2, 16, 1...  7.62 us
    ppermute x3, starting transfers between devices, on_device(): lax.ppermute(image, 'date', perm)  3.51 us
    pallas_call x1, Pallas kernels, compress_range(): pl.pallas_call(range_kernel, out_shape=jax.ShapeDtypeStruct((128, 16, 128...  3.39 us
    ppermute x3, waiting for transfers between devices, on_device(): lax.ppermute(image, 'date', perm)  3.2 us
    pallas_call x1, Pallas kernels, prepare(): pl.pallas_call(prepare_kernel, out_shape=(pltpu.VMEM((4, 8, 128, 128), F3...  3 us
    pallas_call x1, Pallas kernels, focus_columns(): pl.pallas_call(focus_kernel, out_shape=jax.ShapeDtypeStruct((2, ROWS, A),...  2.54 us
  transfers between devices with their start and end apart: 6, of which 3 were waited for; matrix products, arithmetic and copies ran while one was open for 0% of the time, Pallas kernels for 30%

profile of v2, /device:TPU:1, one launch (start us, length us, event | category | flops | bytes accessed | tf_op | source)
XLA Modules:
  0.0 51.1 jit_solution(1503790591518676141)
XLA Ops:
  0.0 3.4 %compress_range.1 = bf16[128,16,128]{2,1,0:T(8,128)(2,1)} custom-call(bf16[2,16,4096]{2,1,0:T(8,128)(2,1)} %raw_hbm.1, f32[32,128]{1,0:T(8,128)} %bitcast.3, f32[2,32,128]{2,1,0:T(8,128)} %constant.14.clone.twist_hbm, bf16[256,512]{1,0:T(8,128)(2,1)} %constant.15.clone.fwd_hbm, bf16[256,512]{1,0:T(8,128)(2,1)} %constant.16.clone.bwd_hbm), custom_call_target="tpu_custom_call" | custom-call | flops 400000000 | bytes 2000000 | tf_op jit(solution)/shard_map/compress_range/pallas_call | solution.py:217
  3.4 1.5 %collective-permute-start.1 = (bf16[2,2,512,2048]{3,2,1,0:T(8,128)(2,1)}, bf16[2,2,512,2048]{3,2,1,0:T(8,128)(2,1)}, u32[]{:S(2)}, u32[]{:S(2)}) collective-permute-start(bf16[2,2,512,2048]{3,2,1,0:T(8,128)(2,1)} %own), channel_id=1, source_target_pairs={{0,1},{1,0},{2,3},{3,2},{4,5},{5,4},{6,7},{7,6},{8,9},{9,8},{10,11... | collective-permute-start | bytes 25165832 | tf_op jit(solution)/shard_map/ppermute | solution.py:560
  4.9 10.2 %all-to-all-start = ((bf16[128,16,128]{2,1,0:T(8,128)(2,1)}), bf16[128,16,128]{2,1,0:T(8,128)(2,1)S(1)}, u32[]{:S(2)}, u32[]{:S(2)}) async-start(bf16[128,16,128]{2,1,0:T(8,128)(2,1)} %compress_range.1), calls=%async_computation | async-start | bytes 1048576 | tf_op jit(solution)/shard_map/all_to_all | solution.py:559
  15.1 3.0 %prepare.1 = (f32[4,8,128,128]{3,2,1,0:T(8,128)S(1)}, bf16[512,512]{1,0:T(8,128)(2,1)S(1)}, f32[2,24,128]{2,1,0:T(8,128)S(1)}) custom-call(bf16[512,2048]{1,0:T(8,128)(2,1)} %angle_hbm, f32[2,8,128,128]{3,2,1,0:T(8,128)} %constant.17.clone.twist_hbm, bf16[512,512]{1,0:T(8,128)(2,1)} %constant.18.clone.mats_hbm, f32[2,24,128]{2,1,0:T(8,128)} %constant.19.clone.last_hbm), custom_call_target="tpu_custom_call" | custom-call | flops 10000000 | bytes 8000000 | tf_op jit(solution)/shard_map/prepare/pallas_call | solution.py:259
  18.1 10.8 %all-to-all-done.lines = bf16[128,16,128]{2,1,0:T(8,128)(2,1)S(1)} async-done(((bf16[128,16,128]{2,1,0:T(8,128)(2,1)}), bf16[128,16,128]{2,1,0:T(8,128)(2,1)S(1)}, u32[]{:S(2)}, u32[]{:S(2)}) %all-to-all-start) | async-done | bytes 524320 | tf_op jit(solution)/shard_map/all_to_all | solution.py:559
  28.9 2.5 %focus_columns.1.image = bf16[2,64,2048]{2,1,0:T(8,128)(2,1)S(1)} custom-call(bf16[128,16,128]{2,1,0:T(8,128)(2,1)S(1)} %all-to-all-done.lines, f32[4,8,128,128]{3,2,1,0:T(8,128)S(1)} %get-tuple-element.19.factors, bf16[512,512]{1,0:T(8,128)(2,1)S(1)} %get-tuple-element.20.mats, f32[2,24,128]{2,1,0:T(8,128)S(1)} %get-tuple-element.21.last), custom_call_target="tpu_custom_call" | custom-call | flops 1000000000 | bytes 4000000 | tf_op jit(solution)/shard_map/focus_columns/pallas_call | solution.py:329
  31.4 0.4 collective-permute-start.3
  31.8 0.5 %collective-permute-start.2 = (bf16[2,64,2048]{2,1,0:T(8,128)(2,1)S(1)}, bf16[2,64,2048]{2,1,0:T(8,128)(2,1)S(1)}, u32[]{:S(2)}, u32[]{:S(2)}) collective-permute-start(bf16[2,64,2048]{2,1,0:T(8,128)(2,1)S(1)} %focus_columns.1.image), channel_id=1, source_target_pairs={{0,8},{1,9},{2,10},{3,11},{4,12},{5,13},{6,14},{7,15},{8,0},{9,1},... | collective-permute-start | bytes 1572872 | tf_op jit(solution)/shard_map/ppermute | solution.py:562
  32.3 2.6 %collective-permute-start = (bf16[2,64,2048]{2,1,0:T(8,128)(2,1)S(1)}, bf16[2,64,2048]{2,1,0:T(8,128)(2,1)S(1)}, u32[]{:S(2)}, u32[]{:S(2)}) collective-permute-start(bf16[2,64,2048]{2,1,0:T(8,128)(2,1)S(1)} %focus_columns.1.image), channel_id=1, source_target_pairs={{0,6},{1,7},{2,0},{3,1},{4,2},{5,3},{6,4},{7,5},{8,14},{9,15},{10,... | collective-permute-start | bytes 1572872 | tf_op jit(solution)/shard_map/ppermute | solution.py:562
  34.9 0.0 collective-permute-done.1.other
  34.9 7.6 %cross_first.1 = (f32[4,2,16,128]{3,2,1,0:T(8,128)S(1)}, bf16[4,2,192,2048]{3,2,1,0:T(8,128)(2,1)S(1)}, f32[3,4,16,128]{3,2,1,0:T(8,128)S(1)}, bf16[2048,128]{1,0:T(8,128)(2,1)S(1)}) custom-call(bf16[2,64,2048]{2,1,0:T(8,128)(2,1)S(1)} %focus_columns.1.image, bf16[2,2,512,2048]{3,2,1,0:T(8,128)(2,1)} %own, ...), custom_call_target="tpu_custom_call" | custom-call | flops 1000000000 | bytes 8000000 | tf_op jit(solution)/shard_map/cross_first/pallas_call | solution.py:426
  42.6 3.2 %collective-permute-done.3.image = bf16[2,64,2048]{2,1,0:T(8,128)(2,1)S(1)} collective-permute-done((bf16[2,64,2048]{2,1,0:T(8,128)(2,1)S(1)}, bf16[2,64,2048]{2,1,0:T(8,128)(2,1)S(1)}, u32[]{:S(2)}, u32[]{:S(2)}) %collective-permute-start.3) | collective-permute-done | bytes 524320 | tf_op jit(solution)/shard_map/ppermute | solution.py:562
  45.8 0.8 %cross_block.3.part2 = f32[4,2,16,128]{3,2,1,0:T(8,128)S(1)} custom-call(bf16[2,64,2048]{2,1,0:T(8,128)(2,1)S(1)} %collective-permute-done.3.image, bf16[4,2,192,2048]{3,2,1,0:T(8,128)(2,1)S(1)} %get-tuple-element.23.held, f32[3,4,16,128]{3,2,1,0:T(8,128)S(1)} %get-tuple-element.24.old_scales, bf16[2048,128]{1,0:T(8,128)(2,1)S(1)} %get-tuple-element.25.pooling), custom_call_target="tpu_custom_call" | custom-call | flops 100000000 | bytes 4000000 | tf_op jit(solution)/shard_map/cross_block/pallas_call | solution.py:456
  46.6 0.0 collective-permute-done.2.image
  46.6 0.8 %cross_block.2.part1 = f32[4,2,16,128]{3,2,1,0:T(8,128)S(1)} custom-call(bf16[2,64,2048]{2,1,0:T(8,128)(2,1)S(1)} %collective-permute-done.2.image, bf16[4,2,192,2048]{3,2,1,0:T(8,128)(2,1)S(1)} %get-tuple-element.23.held, f32[3,4,16,128]{3,2,1,0:T(8,128)S(1)} %get-tuple-element.24.old_scales, bf16[2048,128]{1,0:T(8,128)(2,1)S(1)} %get-tuple-element.25.pooling), custom_call_target="tpu_custom_call" | custom-call | flops 100000000 | bytes 4000000 | tf_op jit(solution)/shard_map/cross_block/pallas_call | solution.py:456
  47.4 0.0 collective-permute-done.image
  47.5 0.0 copy-start
  47.5 0.5 %cross_others.1 = (f32[2,2,64,128]{3,2,1,0:T(8,128)S(1)}, f32[16,128]{1,0:T(8,128)S(1)}) custom-call(bf16[2,64,2048]{2,1,0:T(8,128)(2,1)S(1)} %collective-permute-done.image, bf16[4,2,192,2048]{3,2,1,0:T(8,128)(2,1)S(1)} %get-tuple-element.23.held, f32[3,4,16,128]{3,2,1,0:T(8,128)S(1)} %get-tuple-element.24.old_scales, ...), custom_call_target="tpu_custom_call" | custom-call | flops 100000000 | bytes 4000000 | tf_op jit(solution)/shard_map/cross_others/pallas_call | solution.py:485
  48.0 1.4 %collective-permute-start.4 = (f32[2,2,64,128]{3,2,1,0:T(8,128)S(1)}, f32[2,2,64,128]{3,2,1,0:T(8,128)S(1)}, u32[]{:S(2)}, u32[]{:S(2)}) collective-permute-start(f32[2,2,64,128]{3,2,1,0:T(8,128)S(1)} %get-tuple-element.28), channel_id=1, source_target_pairs={{0,1},{1,0},{2,3},{3,2},{4,5},{5,4},{6,7},{7,6},{8,9},{9,8},{10,11... | collective-permute-start | bytes 393224 | tf_op jit(solution)/shard_map/ppermute | solution.py:566
  49.4 0.5 cross_own.1.mine
  49.8 0.5 %collective-permute-done.4.received = f32[2,2,64,128]{3,2,1,0:T(8,128)S(1)} collective-permute-done((f32[2,2,64,128]{3,2,1,0:T(8,128)S(1)}, f32[2,2,64,128]{3,2,1,0:T(8,128)S(1)}, u32[]{:S(2)}, u32[]{:S(2)}) %collective-permute-start.4) | collective-permute-done | bytes 131104 | tf_op jit(solution)/shard_map/ppermute | solution.py:566
  50.3 0.0 copy-done
  50.4 0.7 %assemble.1 = f32[2,2,128,128]{3,2,1,0:T(8,128)} custom-call(s32[1,128]{1,0:T(1,128)S(1)} %broadcast_in_dim.3.order, f32[2,2,64,128]{3,2,1,0:T(8,128)S(1)} %cross_own.1.mine, f32[2,2,64,128]{3,2,1,0:T(8,128)S(1)} %collective-permute-done.4.received), custom_call_target="tpu_custom_call" | custom-call | flops 1000000 | bytes 1000000 | tf_op jit(solution)/shard_map/assemble/pallas_call | solution.py:531
  (1 shorter events, 0.0 us)
Async XLA Ops:
  3.4 31.5 %collective-permute-start.1 = (bf16[2,2,512,2048]{3,2,1,0:T(8,128)(2,1)}, bf16[2,2,512,2048]{3,2,1,0:T(8,128)(2,1)}, u32[]{:S(2)}, u32[]{:S(2)}) collective-permute-start(bf16[2,2,512,2048]{3,2,1,0:T(8,128)(2,1)} %own), channel_id=1, source_target_pairs={{0,1},{1,0},{2,3},{3,2},{4,5},{5,4},{6,7},{7,6},{8,9},{9,8},{10,11... | collective-permute-start | bytes 25165832 | tf_op jit(solution)/shard_map/ppermute | solution.py:560
  4.9 24.0 %all-to-all-start = ((bf16[128,16,128]{2,1,0:T(8,128)(2,1)}), bf16[128,16,128]{2,1,0:T(8,128)(2,1)S(1)}, u32[]{:S(2)}, u32[]{:S(2)}) async-start(bf16[128,16,128]{2,1,0:T(8,128)(2,1)} %compress_range.1), calls=%async_computation | async-start | bytes 1048576 | tf_op jit(solution)/shard_map/all_to_all | solution.py:559
  31.4 14.3 %collective-permute-start.3 = (bf16[2,64,2048]{2,1,0:T(8,128)(2,1)S(1)}, bf16[2,64,2048]{2,1,0:T(8,128)(2,1)S(1)}, u32[]{:S(2)}, u32[]{:S(2)}) collective-permute-start(bf16[2,64,2048]{2,1,0:T(8,128)(2,1)S(1)} %focus_columns.1.image), channel_id=1, source_target_pairs={{0,2},{1,3},{2,4},{3,5},{4,6},{5,7},{6,0},{7,1},{8,10},{9,11},{10,... | collective-permute-start | bytes 1572872 | tf_op jit(solution)/shard_map/ppermute | solution.py:562
  31.8 14.8 %collective-permute-start.2 = (bf16[2,64,2048]{2,1,0:T(8,128)(2,1)S(1)}, bf16[2,64,2048]{2,1,0:T(8,128)(2,1)S(1)}, u32[]{:S(2)}, u32[]{:S(2)}) collective-permute-start(bf16[2,64,2048]{2,1,0:T(8,128)(2,1)S(1)} %focus_columns.1.image), channel_id=1, source_target_pairs={{0,8},{1,9},{2,10},{3,11},{4,12},{5,13},{6,14},{7,15},{8,0},{9,1},... | collective-permute-start | bytes 1572872 | tf_op jit(solution)/shard_map/ppermute | solution.py:562
  32.3 15.1 %collective-permute-start = (bf16[2,64,2048]{2,1,0:T(8,128)(2,1)S(1)}, bf16[2,64,2048]{2,1,0:T(8,128)(2,1)S(1)}, u32[]{:S(2)}, u32[]{:S(2)}) collective-permute-start(bf16[2,64,2048]{2,1,0:T(8,128)(2,1)S(1)} %focus_columns.1.image), channel_id=1, source_target_pairs={{0,6},{1,7},{2,0},{3,1},{4,2},{5,3},{6,4},{7,5},{8,14},{9,15},{10,... | collective-permute-start | bytes 1572872 | tf_op jit(solution)/shard_map/ppermute | solution.py:562
  47.5 2.9 %copy-start = (s32[2]{0:T(128)S(1)}, s32[2]{0:T(128)}, u32[]{:S(2)}) copy-start(s32[2]{0:T(128)} %param.16) | copy-start | bytes 28
  48.0 2.3 %collective-permute-start.4 = (f32[2,2,64,128]{3,2,1,0:T(8,128)S(1)}, f32[2,2,64,128]{3,2,1,0:T(8,128)S(1)}, u32[]{:S(2)}, u32[]{:S(2)}) collective-permute-start(f32[2,2,64,128]{3,2,1,0:T(8,128)S(1)} %get-tuple-element.28), channel_id=1, source_target_pairs={{0,1},{1,0},{2,3},{3,2},{4,5},{5,4},{6,7},{7,6},{8,9},{9,8},{10,11... | collective-permute-start | bytes 393224 | tf_op jit(solution)/shard_map/ppermute | solution.py:566

commit v3 on v2

--- a/solution.py
+++ b/solution.py
@@ -79,8 +79,10 @@
     t = np.arange(128)
     k1 = 4 * (t % 32) + t // 32
     angle = 2 * np.pi * np.outer(t, k1) / 128
-    fwd = np.concatenate(split(real_form(angle, -1)), axis=1)
-    bwd = np.concatenate(split(real_form(angle.T, 1)), axis=1)
+    fwd, bwd = (
+        np.concatenate([high, high, low], axis=0)
+        for high, low in (split(real_form(angle, -1)), split(real_form(angle.T, 1)))
+    )
     twist = 2 * np.pi * np.outer(np.arange(32), t) / R
     return np.stack([np.cos(twist), -np.sin(twist)]).astype(np.float32), fwd, bwd
 
@@ -117,10 +119,16 @@
     return high, (x - high.astype(F32)).astype(BF16)
 
 
+def keep(target, rows, re, im):
+    (re_high, re_low), (im_high, im_low) = halves(re), halves(im)
+    target[rows, 0:128] = re_high
+    target[rows, 128:256] = im_high
+    target[rows, 256:384] = re_low
+    target[rows, 384:512] = im_low
+
+
 def dot_split(x, table):
-    high, low = halves(x)
-    n = table.shape[1] // 2
-    return dot(high, table[:, :n]) + dot(low, table[:, :n]) + dot(high, table[:, n:])
+    return dot(x[...], table[0:512]) + dot(x[:, 0:256], table[512:768])
 
 
 def params(mib):
@@ -152,7 +160,7 @@
     date = lax.axis_index("date")
     zh, y, core = lax.shift_right_logical(date, 3), lax.shift_right_logical(date, 1) & 3, date & 1
     block = (y + 2 * zh) & 3
-    return core, (block, (block + 2) & 3, (block + 3) & 3, (block + 1) & 3)
+    return core, (block, (block + 3) & 3, (block + 2) & 3, (block + 1) & 3)
 
 
 def archive_rows(n):
@@ -178,17 +186,15 @@
     ]
     for k0, value in enumerate(fft(values, -1)):
         re, im = cmul(value, (twist[0, k0 : k0 + 1, :], twist[1, k0 : k0 + 1, :]))
-        a[16 * k0 : 16 * k0 + 16, 0:128] = re
-        a[16 * k0 : 16 * k0 + 16, 128:256] = im
+        keep(a, slice(16 * k0, 16 * k0 + 16), re, im)
     copies[3].wait()
-    b[...] = dot_split(a[...], fwd)
+    b[...] = dot_split(a, fwd)
     for k0 in range(32):
         rows = slice(16 * k0, 16 * k0 + 16)
         re, im = cmul((b[rows, 0:128], b[rows, 128:256]), (cosine[k0 : k0 + 1], sine[k0 : k0 + 1]))
-        a[rows, 0:128] = re
-        a[rows, 128:256] = im
+        keep(a, rows, re, im)
     copies[4].wait()
-    b[...] = dot_split(a[...], bwd)
+    b[...] = dot_split(a, bwd)
     values = []
     for k0 in range(32):
         rows = slice(16 * k0, 16 * k0 + 16)
@@ -197,6 +203,7 @@
         )
     left = lax.broadcasted_iota(jnp.int32, (8, 128), 1) < 64
     for q, value in enumerate(fft(values, 1)):
+        pixel, core = q // 4, (q // 2) % 2
         for half in range(2):
             parts = []
             for part in value:
@@ -206,7 +213,7 @@
                 else:
                     parts.append(jnp.where(left, pltpu.roll(low, 64, 1), high))
             message = jnp.concatenate(parts, axis=0).astype(BF16)
-            pixel, core, block = q // 4, (q // 2) % 2, 2 * (q % 2) + half
+            block = 2 * (q % 2) + half
             for zh in range(2):
                 y = (block + 2 * zh) % 4
                 out[pixel * 16 + zh * 8 + y * 2 + core] = message
@@ -223,9 +230,9 @@
             pltpu.VMEM((2, 16, R), BF16),
             pltpu.VMEM((32, 128), F32),
             pltpu.VMEM((2, 32, 128), F32),
-            pltpu.VMEM((256, 512), BF16),
-            pltpu.VMEM((256, 512), BF16),
-            pltpu.VMEM((512, 256), F32),
+            pltpu.VMEM((768, 256), BF16),
+            pltpu.VMEM((768, 256), BF16),
+            pltpu.VMEM((512, 512), BF16),
             pltpu.VMEM((512, 256), F32),
             pltpu.SemaphoreType.DMA((5,)),
         ],
@@ -294,7 +301,7 @@
             filtered[1, k, rows, :] = im
         return carry
 
-    lax.fori_loop(0, 16, tile, 0, unroll=4)
+    lax.fori_loop(0, 16, tile, 0, unroll=True)
 
     for kappa in range(16):
         block = jnp.concatenate(
@@ -469,51 +476,56 @@
     target[:, :, pl.ds(pl.multiple_of(place()[1][n] * 16, 16), 16), :] = parts
 
 
-def other_kernel(image, held, old_scales, pooling, part0, part1, part2, out, new_scale, products, pooled):
-    for date in range(2):
-        cross_products(products, 2 * date * ROWS, image, held.at[2 + date], block_rows(2))
-    power_products(products, 4 * ROWS, image, ALL_ROWS)
-    for n, part in enumerate((part0, part1, part2)):
+def other_kernel(image1, image2, held, old_scales, pooling, part0, part1, out, new_scale, products, pooled):
+    for n, image in enumerate((image1, image2)):
+        for date in range(2):
+            cross_products(products, (4 * n + 2 * date) * ROWS, image, held.at[2 + date], block_rows(n + 1))
+        power_products(products, (8 + n) * ROWS, image, ALL_ROWS)
+    for n, part in enumerate((part0, part1)):
         put(n, out, part[2:4])
-    sums = pool(products, pooling, pooled, 5)
-    new = inverse_root(sums[4])
-    new_scale[...] = new
-    put(3, out, sums[0:4].reshape(2, 2, 16, 128) * (new * old_scales[2, 2:4])[:, None])
-
-
-def cross_others(image, held, old_scales, pooling, parts):
+    sums = pool(products, pooling, pooled, 10)
+    for n in range(2):
+        new = inverse_root(sums[8 + n])
+        new_scale[n] = new
+        put(n + 2, out, sums[4 * n : 4 * n + 4].reshape(2, 2, 16, 128) * (new * old_scales[n + 1, 2:4])[:, None])
+
+
+def cross_others(images, held, old_scales, pooling, parts):
     return pl.pallas_call(
         other_kernel,
-        out_shape=(jax.ShapeDtypeStruct((2, 2, 64, 128), F32), jax.ShapeDtypeStruct((16, 128), F32)),
+        out_shape=(jax.ShapeDtypeStruct((2, 2, 64, 128), F32), jax.ShapeDtypeStruct((2, 16, 128), F32)),
         in_specs=[VMEM] * 7,
         out_specs=(VMEM, VMEM),
-        scratch_shapes=scratch(5),
+        scratch_shapes=scratch(10),
         compiler_params=params(24),
         cost_estimate=cost(10**8, 4 * 10**6),
         name="cross_others",
-    )(image, held, old_scales, pooling, *parts)
-
-
-def own_kernel(image, held, old_scales, pooling, part0, part1, part2, new_scale, out, products, pooled):
-    for date in range(2):
-        cross_products(products, 2 * date * ROWS, image, held.at[date], block_rows(2))
-    for n, part in enumerate((part0, part1, part2)):
+    )(*images, held, old_scales, pooling, *parts)
+
+
+def own_kernel(image1, image2, held, old_scales, pooling, part0, part1, new_scale, out, products, pooled):
+    for n, image in enumerate((image1, image2)):
+        for date in range(2):
+            cross_products(products, (4 * n + 2 * date) * ROWS, image, held.at[date], block_rows(n + 1))
+    for n, part in enumerate((part0, part1)):
         put(n, out, part[0:2])
-    sums = pool(products, pooling, pooled, 4)
-    put(3, out, sums.reshape(2, 2, 16, 128) * (new_scale[...] * old_scales[2, 0:2])[:, None])
-
-
-def cross_own(image, held, old_scales, pooling, parts, new_scale):
+    sums = pool(products, pooling, pooled, 8)
+    for n in range(2):
+        scale = (new_scale[n] * old_scales[n + 1, 0:2])[:, None]
+        put(n + 2, out, sums[4 * n : 4 * n + 4].reshape(2, 2, 16, 128) * scale)
+
+
+def cross_own(images, held, old_scales, pooling, parts, new_scale):
     return pl.pallas_call(
         own_kernel,
         out_shape=jax.ShapeDtypeStruct((2, 2, 64, 128), F32),
         in_specs=[VMEM] * 8,
         out_specs=VMEM,
-        scratch_shapes=scratch(4),
+        scratch_shapes=scratch(8),
         compiler_params=params(24),
         cost_estimate=cost(10**8, 4 * 10**6),
         name="cross_own",
-    )(image, held, old_scales, pooling, *parts, new_scale)
+    )(*images, held, old_scales, pooling, *parts, new_scale)
 
 
 def final_kernel(order, mine, received, out):
@@ -559,12 +571,12 @@
     lines = lax.all_to_all(messages, ALL, 0, 0, tiled=True)
     other_archive = lax.ppermute(archive, "date", OTHER_CORE)
     image = focus_columns(lines, *prepare(azimuth_phase))
-    images = [lax.ppermute(image, "date", perm) for perm in (OTHER_Z, NEXT_Y, LAST_Y)]
+    images = [lax.ppermute(image, "date", perm) for perm in (NEXT_Y, OTHER_Z, LAST_Y)]
     first, *kept = cross_first(image, archive, other_archive, jnp.asarray(pooling_table()))
-    parts = [first] + [cross_block(n, images[n], *kept) for n in range(2)]
-    others, new_scale = cross_others(images[2], *kept, parts)
+    parts = [first, cross_block(0, images[0], *kept)]
+    others, new_scale = cross_others(images[1:], *kept, parts)
     received = lax.ppermute(others, "date", OTHER_CORE)
-    mine = cross_own(images[2], *kept, parts, new_scale)
+    mine = cross_own(images[1:], *kept, parts, new_scale)
     return assemble(date_order, mine, received)
 
 

time: 51.3 us -> 50.7 us (0.988)
    pallas_call x2 -> x1, Pallas kernels: 1.66 us -> 0.82 us  [cross_block(): pl.pallas_call(partial(block_kernel, n), out_shape=jax.ShapeDtypeStruct((...]
  transfers between devices with their start and end apart: 6 -> 6, of which waited for: 3 -> 3; matrix products, arithmetic and copies ran while one was open for 0% -> 0% of each run, Pallas kernels for 30% -> 29%
where the time goes in v3:
time: 50.7 us; the launch traced here: 50.5 us
  Pallas kernels  19.6 us (39%)
  starting transfers between devices  16.6 us (33%)
  waiting for transfers between devices  14.2 us (28%)
    all_to_all x1, waiting for transfers between devices, on_device(): lines = lax.all_to_all(messages, ALL, 0, 0, tiled=True)  10.8 us
    all_to_all x1, starting transfers between devices, on_device(): lines = lax.all_to_all(messages, ALL, 0, 0, tiled=True)  10.2 us
    pallas_call x1, Pallas kernels, cross_first(): pl.pallas_call(first_kernel, out_shape=(jax.ShapeDtypeStruct((4, 2, 16, 1...  7.6 us
    ppermute x3, starting transfers between devices, on_device(): lax.ppermute(image, 'date', perm)  3.51 us
    pallas_call x1, Pallas kernels, compress_range(): pl.pallas_call(range_kernel, out_shape=jax.ShapeDtypeStruct((128, 16, 128...  3.44 us
    ppermute x3, waiting for transfers between devices, on_device(): lax.ppermute(image, 'date', perm)  3.22 us
    pallas_call x1, Pallas kernels, prepare(): pl.pallas_call(prepare_kernel, out_shape=(pltpu.VMEM((4, 8, 128, 128), F3...  3 us
    pallas_call x1, Pallas kernels, focus_columns(): pl.pallas_call(focus_kernel, out_shape=jax.ShapeDtypeStruct((2, ROWS, A),...  2.35 us
  transfers between devices with their start and end apart: 6, of which 3 were waited for; matrix products, arithmetic and copies ran while one was open for 0% of the time, Pallas kernels for 29%

profile of v3, /device:TPU:1, one launch (start us, length us, event | category | flops | bytes accessed | tf_op | source)
XLA Modules:
  0.0 50.5 jit_solution(12863950562562243887)
XLA Ops:
  0.0 3.4 %compress_range.1 = bf16[128,16,128]{2,1,0:T(8,128)(2,1)} custom-call(bf16[2,16,4096]{2,1,0:T(8,128)(2,1)} %raw_hbm.1, f32[32,128]{1,0:T(8,128)} %bitcast.3, f32[2,32,128]{2,1,0:T(8,128)} %constant.14.clone.twist_hbm, bf16[768,256]{1,0:T(8,128)(2,1)} %constant.15.clone.fwd_hbm, bf16[768,256]{1,0:T(8,128)(2,1)} %constant.16.clone.bwd_hbm), custom_call_target="tpu_custom_call" | custom-call | flops 400000000 | bytes 2000000 | tf_op jit(solution)/shard_map/compress_range/pallas_call | solution.py:224
  3.5 1.5 %collective-permute-start.2 = (bf16[2,2,512,2048]{3,2,1,0:T(8,128)(2,1)}, bf16[2,2,512,2048]{3,2,1,0:T(8,128)(2,1)}, u32[]{:S(2)}, u32[]{:S(2)}) collective-permute-start(bf16[2,2,512,2048]{3,2,1,0:T(8,128)(2,1)} %own), channel_id=1, source_target_pairs={{0,1},{1,0},{2,3},{3,2},{4,5},{5,4},{6,7},{7,6},{8,9},{9,8},{10,11... | collective-permute-start | bytes 25165832 | tf_op jit(solution)/shard_map/ppermute | solution.py:572
  5.0 10.2 %all-to-all-start = ((bf16[128,16,128]{2,1,0:T(8,128)(2,1)}), bf16[128,16,128]{2,1,0:T(8,128)(2,1)S(1)}, u32[]{:S(2)}, u32[]{:S(2)}) async-start(bf16[128,16,128]{2,1,0:T(8,128)(2,1)} %compress_range.1), calls=%async_computation | async-start | bytes 1048576 | tf_op jit(solution)/shard_map/all_to_all | solution.py:571
  15.2 3.0 %prepare.1 = (f32[4,8,128,128]{3,2,1,0:T(8,128)S(1)}, bf16[512,512]{1,0:T(8,128)(2,1)S(1)}, f32[2,24,128]{2,1,0:T(8,128)S(1)}) custom-call(bf16[512,2048]{1,0:T(8,128)(2,1)} %angle_hbm, f32[2,8,128,128]{3,2,1,0:T(8,128)} %constant.17.clone.twist_hbm, bf16[512,512]{1,0:T(8,128)(2,1)} %constant.18.clone.mats_hbm, f32[2,24,128]{2,1,0:T(8,128)} %constant.19.clone.last_hbm), custom_call_target="tpu_custom_call" | custom-call | flops 10000000 | bytes 8000000 | tf_op jit(solution)/shard_map/prepare/pallas_call | solution.py:266
  18.2 10.8 %all-to-all-done.lines = bf16[128,16,128]{2,1,0:T(8,128)(2,1)S(1)} async-done(((bf16[128,16,128]{2,1,0:T(8,128)(2,1)}), bf16[128,16,128]{2,1,0:T(8,128)(2,1)S(1)}, u32[]{:S(2)}, u32[]{:S(2)}) %all-to-all-start) | async-done | bytes 524320 | tf_op jit(solution)/shard_map/all_to_all | solution.py:571
  28.9 2.3 %focus_columns.1.image = bf16[2,64,2048]{2,1,0:T(8,128)(2,1)S(1)} custom-call(bf16[128,16,128]{2,1,0:T(8,128)(2,1)S(1)} %all-to-all-done.lines, f32[4,8,128,128]{3,2,1,0:T(8,128)S(1)} %get-tuple-element.19.factors, bf16[512,512]{1,0:T(8,128)(2,1)S(1)} %get-tuple-element.20.mats, f32[2,24,128]{2,1,0:T(8,128)S(1)} %get-tuple-element.21.last), custom_call_target="tpu_custom_call" | custom-call | flops 1000000000 | bytes 4000000 | tf_op jit(solution)/shard_map/focus_columns/pallas_call | solution.py:336
  31.3 0.4 collective-permute-start.3
  31.7 0.5 %collective-permute-start = (bf16[2,64,2048]{2,1,0:T(8,128)(2,1)S(1)}, bf16[2,64,2048]{2,1,0:T(8,128)(2,1)S(1)}, u32[]{:S(2)}, u32[]{:S(2)}) collective-permute-start(bf16[2,64,2048]{2,1,0:T(8,128)(2,1)S(1)} %focus_columns.1.image), channel_id=1, source_target_pairs={{0,8},{1,9},{2,10},{3,11},{4,12},{5,13},{6,14},{7,15},{8,0},{9,1},... | collective-permute-start | bytes 1572872 | tf_op jit(solution)/shard_map/ppermute | solution.py:574
  32.2 2.6 %collective-permute-start.1 = (bf16[2,64,2048]{2,1,0:T(8,128)(2,1)S(1)}, bf16[2,64,2048]{2,1,0:T(8,128)(2,1)S(1)}, u32[]{:S(2)}, u32[]{:S(2)}) collective-permute-start(bf16[2,64,2048]{2,1,0:T(8,128)(2,1)S(1)} %focus_columns.1.image), channel_id=1, source_target_pairs={{0,6},{1,7},{2,0},{3,1},{4,2},{5,3},{6,4},{7,5},{8,14},{9,15},{10,... | collective-permute-start | bytes 1572872 | tf_op jit(solution)/shard_map/ppermute | solution.py:574
  34.8 0.0 collective-permute-done.2.other
  34.8 7.6 %cross_first.1 = (f32[4,2,16,128]{3,2,1,0:T(8,128)S(1)}, bf16[4,2,192,2048]{3,2,1,0:T(8,128)(2,1)S(1)}, f32[3,4,16,128]{3,2,1,0:T(8,128)S(1)}, bf16[2048,128]{1,0:T(8,128)(2,1)S(1)}) custom-call(bf16[2,64,2048]{2,1,0:T(8,128)(2,1)S(1)} %focus_columns.1.image, bf16[2,2,512,2048]{3,2,1,0:T(8,128)(2,1)} %own, ...), custom_call_target="tpu_custom_call" | custom-call | flops 1000000000 | bytes 8000000 | tf_op jit(solution)/shard_map/cross_first/pallas_call | solution.py:433
  42.4 3.2 %collective-permute-done.3.image = bf16[2,64,2048]{2,1,0:T(8,128)(2,1)S(1)} collective-permute-done((bf16[2,64,2048]{2,1,0:T(8,128)(2,1)S(1)}, bf16[2,64,2048]{2,1,0:T(8,128)(2,1)S(1)}, u32[]{:S(2)}, u32[]{:S(2)}) %collective-permute-start.3) | collective-permute-done | bytes 524320 | tf_op jit(solution)/shard_map/ppermute | solution.py:574
  45.6 0.8 %cross_block.1.part1 = f32[4,2,16,128]{3,2,1,0:T(8,128)S(1)} custom-call(bf16[2,64,2048]{2,1,0:T(8,128)(2,1)S(1)} %collective-permute-done.3.image, bf16[4,2,192,2048]{3,2,1,0:T(8,128)(2,1)S(1)} %get-tuple-element.23.held, f32[3,4,16,128]{3,2,1,0:T(8,128)S(1)} %get-tuple-element.24.old_scales, bf16[2048,128]{1,0:T(8,128)(2,1)S(1)} %get-tuple-element.25.pooling), custom_call_target="tpu_custom_call" | custom-call | flops 100000000 | bytes 4000000 | tf_op jit(solution)/shard_map/cross_block/pallas_call | solution.py:463
  46.4 0.0 collective-permute-done.image1
  46.4 0.0 collective-permute-done.1.image2
  46.5 0.0 copy-start
  46.5 0.9 %cross_others.1 = (f32[2,2,64,128]{3,2,1,0:T(8,128)S(1)}, f32[2,16,128]{2,1,0:T(8,128)S(1)}) custom-call(bf16[2,64,2048]{2,1,0:T(8,128)(2,1)S(1)} %collective-permute-done.image1, bf16[2,64,2048]{2,1,0:T(8,128)(2,1)S(1)} %collective-permute-done.1.image2, bf16[4,2,192,2048]{3,2,1,0:T(8,128)(2,1)S(1)} %get-tuple-element.23.held, ...), custom_call_target="tpu_custom_call" | custom-call | flops 100000000 | bytes 4000000 | tf_op jit(solution)/shard_map/cross_others/pallas_call | solution.py:494
  47.4 1.4 %collective-permute-start.4 = (f32[2,2,64,128]{3,2,1,0:T(8,128)S(1)}, f32[2,2,64,128]{3,2,1,0:T(8,128)S(1)}, u32[]{:S(2)}, u32[]{:S(2)}) collective-permute-start(f32[2,2,64,128]{3,2,1,0:T(8,128)S(1)} %get-tuple-element.28), channel_id=1, source_target_pairs={{0,1},{1,0},{2,3},{3,2},{4,5},{5,4},{6,7},{7,6},{8,9},{9,8},{10,11... | collective-permute-start | bytes 393224 | tf_op jit(solution)/shard_map/ppermute | solution.py:578
  48.7 0.8 %cross_own.1.mine = f32[2,2,64,128]{3,2,1,0:T(8,128)S(1)} custom-call(bf16[2,64,2048]{2,1,0:T(8,128)(2,1)S(1)} %collective-permute-done.image1, bf16[2,64,2048]{2,1,0:T(8,128)(2,1)S(1)} %collective-permute-done.1.image2, bf16[4,2,192,2048]{3,2,1,0:T(8,128)(2,1)S(1)} %get-tuple-element.23.held, f32[3,4,16,128]{3,2,1,0:T(8,128)S(1)} %get-tuple-element.24.old_scales, ...), custom_call_target="tpu_custom_call" | custom-call | flops 100000000 | bytes 4000000 | tf_op jit(solution)/shard_map/cross_own/pallas_call | solution.py:519
  49.5 0.2 collective-permute-done.4.received
  49.7 0.0 copy-done
  49.8 0.7 %assemble.1 = f32[2,2,128,128]{3,2,1,0:T(8,128)} custom-call(s32[1,128]{1,0:T(1,128)S(1)} %broadcast_in_dim.3.order, f32[2,2,64,128]{3,2,1,0:T(8,128)S(1)} %cross_own.1.mine, f32[2,2,64,128]{3,2,1,0:T(8,128)S(1)} %collective-permute-done.4.received), custom_call_target="tpu_custom_call" | custom-call | flops 1000000 | bytes 1000000 | tf_op jit(solution)/shard_map/assemble/pallas_call | solution.py:543
  (1 shorter events, 0.0 us)
Async XLA Ops:
  3.5 31.3 %collective-permute-start.2 = (bf16[2,2,512,2048]{3,2,1,0:T(8,128)(2,1)}, bf16[2,2,512,2048]{3,2,1,0:T(8,128)(2,1)}, u32[]{:S(2)}, u32[]{:S(2)}) collective-permute-start(bf16[2,2,512,2048]{3,2,1,0:T(8,128)(2,1)} %own), channel_id=1, source_target_pairs={{0,1},{1,0},{2,3},{3,2},{4,5},{5,4},{6,7},{7,6},{8,9},{9,8},{10,11... | collective-permute-start | bytes 25165832 | tf_op jit(solution)/shard_map/ppermute | solution.py:572
  5.0 24.0 %all-to-all-start = ((bf16[128,16,128]{2,1,0:T(8,128)(2,1)}), bf16[128,16,128]{2,1,0:T(8,128)(2,1)S(1)}, u32[]{:S(2)}, u32[]{:S(2)}) async-start(bf16[128,16,128]{2,1,0:T(8,128)(2,1)} %compress_range.1), calls=%async_computation | async-start | bytes 1048576 | tf_op jit(solution)/shard_map/all_to_all | solution.py:571
  31.3 14.3 %collective-permute-start.3 = (bf16[2,64,2048]{2,1,0:T(8,128)(2,1)S(1)}, bf16[2,64,2048]{2,1,0:T(8,128)(2,1)S(1)}, u32[]{:S(2)}, u32[]{:S(2)}) collective-permute-start(bf16[2,64,2048]{2,1,0:T(8,128)(2,1)S(1)} %focus_columns.1.image), channel_id=1, source_target_pairs={{0,2},{1,3},{2,4},{3,5},{4,6},{5,7},{6,0},{7,1},{8,10},{9,11},{10,... | collective-permute-start | bytes 1572872 | tf_op jit(solution)/shard_map/ppermute | solution.py:574
  31.7 14.7 %collective-permute-start = (bf16[2,64,2048]{2,1,0:T(8,128)(2,1)S(1)}, bf16[2,64,2048]{2,1,0:T(8,128)(2,1)S(1)}, u32[]{:S(2)}, u32[]{:S(2)}) collective-permute-start(bf16[2,64,2048]{2,1,0:T(8,128)(2,1)S(1)} %focus_columns.1.image), channel_id=1, source_target_pairs={{0,8},{1,9},{2,10},{3,11},{4,12},{5,13},{6,14},{7,15},{8,0},{9,1},... | collective-permute-start | bytes 1572872 | tf_op jit(solution)/shard_map/ppermute | solution.py:574
  32.2 14.2 %collective-permute-start.1 = (bf16[2,64,2048]{2,1,0:T(8,128)(2,1)S(1)}, bf16[2,64,2048]{2,1,0:T(8,128)(2,1)S(1)}, u32[]{:S(2)}, u32[]{:S(2)}) collective-permute-start(bf16[2,64,2048]{2,1,0:T(8,128)(2,1)S(1)} %focus_columns.1.image), channel_id=1, source_target_pairs={{0,6},{1,7},{2,0},{3,1},{4,2},{5,3},{6,4},{7,5},{8,14},{9,15},{10,... | collective-permute-start | bytes 1572872 | tf_op jit(solution)/shard_map/ppermute | solution.py:574
  46.5 3.3 %copy-start = (s32[2]{0:T(128)S(1)}, s32[2]{0:T(128)}, u32[]{:S(2)}) copy-start(s32[2]{0:T(128)} %param.16) | copy-start | bytes 28
  47.4 2.4 %collective-permute-start.4 = (f32[2,2,64,128]{3,2,1,0:T(8,128)S(1)}, f32[2,2,64,128]{3,2,1,0:T(8,128)S(1)}, u32[]{:S(2)}, u32[]{:S(2)}) collective-permute-start(f32[2,2,64,128]{3,2,1,0:T(8,128)S(1)} %get-tuple-element.28), channel_id=1, source_target_pairs={{0,1},{1,0},{2,3},{3,2},{4,5},{5,4},{6,7},{7,6},{8,9},{9,8},{10,11... | collective-permute-start | bytes 393224 | tf_op jit(solution)/shard_map/ppermute | solution.py:578

commit v4 on v3

--- a/solution.py
+++ b/solution.py
@@ -160,7 +160,7 @@
     date = lax.axis_index("date")
     zh, y, core = lax.shift_right_logical(date, 3), lax.shift_right_logical(date, 1) & 3, date & 1
     block = (y + 2 * zh) & 3
-    return core, (block, (block + 3) & 3, (block + 2) & 3, (block + 1) & 3)
+    return core, (block, (block + 3 - 2 * core) & 3, (block + 2) & 3, (block + 1 + 2 * core) & 3)
 
 
 def archive_rows(n):
@@ -560,9 +560,11 @@
 
 
 OTHER_CORE = pairs(lambda zh, y, core: (zh, y, 1 - core))
-OTHER_Z = pairs(lambda zh, y, core: (1 - zh, y, core))
-NEXT_Y = pairs(lambda zh, y, core: (zh, y + 1, core))
-LAST_Y = pairs(lambda zh, y, core: (zh, y + 3, core))
+ROUNDS = (
+    pairs(lambda zh, y, core: (zh, y + 3, core) if core else (zh, y + 1, core)),
+    pairs(lambda zh, y, core: (1 - zh, y, core)),
+    pairs(lambda zh, y, core: (zh, y + 1, core) if core else (zh, y + 3, core)),
+)
 
 
 def on_device(raw_echoes, range_phase, azimuth_phase, archive, date_order):
@@ -571,7 +573,7 @@
     lines = lax.all_to_all(messages, ALL, 0, 0, tiled=True)
     other_archive = lax.ppermute(archive, "date", OTHER_CORE)
     image = focus_columns(lines, *prepare(azimuth_phase))
-    images = [lax.ppermute(image, "date", perm) for perm in (NEXT_Y, OTHER_Z, LAST_Y)]
+    images = [lax.ppermute(image, "date", perm) for perm in ROUNDS]
     first, *kept = cross_first(image, archive, other_archive, jnp.asarray(pooling_table()))
     parts = [first, cross_block(0, images[0], *kept)]
     others, new_scale = cross_others(images[1:], *kept, parts)

time: 50.7 us -> 50.9 us (level)
  waiting for transfers between devices: 14.2 us -> 16.4 us
  starting transfers between devices: 16.6 us -> 14.6 us
    ppermute x3, waiting for transfers between devices: 3.22 us -> 5.39 us  [on_device(): images = [lax.ppermute(image, 'date', perm) for perm in ROUNDS]]
    ppermute x3, starting transfers between devices: 3.51 us -> 2.3 us  [on_device(): images = [lax.ppermute(image, 'date', perm) for perm in ROUNDS]]
    ppermute x1, starting transfers between devices: 1.36 us -> 0.59 us  [on_device(): received = lax.ppermute(others, 'date', OTHER_CORE)]
  transfers between devices with their start and end apart: 6 -> 6, of which waited for: 3 -> 5; matrix products, arithmetic and copies ran while one was open for 0% -> 0% of each run, Pallas kernels for 29% -> 29%
where the time goes in v4:
time: 50.9 us; the launch traced here: 50.7 us
  Pallas kernels  19.6 us (39%)
  waiting for transfers between devices  16.4 us (32%)
  starting transfers between devices  14.6 us (29%)
    all_to_all x1, waiting for transfers between devices, on_device(): lines = lax.all_to_all(messages, ALL, 0, 0, tiled=True)  10.8 us
    all_to_all x1, starting transfers between devices, on_device(): lines = lax.all_to_all(messages, ALL, 0, 0, tiled=True)  10.2 us
    pallas_call x1, Pallas kernels, cross_first(): pl.pallas_call(first_kernel, out_shape=(jax.ShapeDtypeStruct((4, 2, 16, 1...  7.6 us
    ppermute x3, waiting for transfers between devices, on_device(): images = [lax.ppermute(image, 'date', perm) for perm in ROUNDS]  5.39 us
    pallas_call x1, Pallas kernels, compress_range(): pl.pallas_call(range_kernel, out_shape=jax.ShapeDtypeStruct((128, 16, 128...  3.44 us
    pallas_call x1, Pallas kernels, prepare(): pl.pallas_call(prepare_kernel, out_shape=(pltpu.VMEM((4, 8, 128, 128), F3...  3 us
    pallas_call x1, Pallas kernels, focus_columns(): pl.pallas_call(focus_kernel, out_shape=jax.ShapeDtypeStruct((2, ROWS, A),...  2.35 us
    ppermute x3, starting transfers between devices, on_device(): images = [lax.ppermute(image, 'date', perm) for perm in ROUNDS]  2.3 us
  transfers between devices with their start and end apart: 6, of which 5 were waited for; matrix products, arithmetic and copies ran while one was open for 0% of the time, Pallas kernels for 29%

profile of v4, /device:TPU:1, one launch (start us, length us, event | category | flops | bytes accessed | tf_op | source)
XLA Modules:
  0.0 50.7 jit_solution(18436169374129857103)
XLA Ops:
  0.0 3.4 %compress_range.1 = bf16[128,16,128]{2,1,0:T(8,128)(2,1)} custom-call(bf16[2,16,4096]{2,1,0:T(8,128)(2,1)} %raw_hbm.1, f32[32,128]{1,0:T(8,128)} %bitcast.3, f32[2,32,128]{2,1,0:T(8,128)} %constant.14.clone.twist_hbm, bf16[768,256]{1,0:T(8,128)(2,1)} %constant.15.clone.fwd_hbm, bf16[768,256]{1,0:T(8,128)(2,1)} %constant.16.clone.bwd_hbm), custom_call_target="tpu_custom_call" | custom-call | flops 400000000 | bytes 2000000 | tf_op jit(solution)/shard_map/compress_range/pallas_call | solution.py:224
  3.5 1.5 %collective-permute-start.2 = (bf16[2,2,512,2048]{3,2,1,0:T(8,128)(2,1)}, bf16[2,2,512,2048]{3,2,1,0:T(8,128)(2,1)}, u32[]{:S(2)}, u32[]{:S(2)}) collective-permute-start(bf16[2,2,512,2048]{3,2,1,0:T(8,128)(2,1)} %own), channel_id=1, source_target_pairs={{0,1},{1,0},{2,3},{3,2},{4,5},{5,4},{6,7},{7,6},{8,9},{9,8},{10,11... | collective-permute-start | bytes 25165832 | tf_op jit(solution)/shard_map/ppermute | solution.py:574
  5.0 10.2 %all-to-all-start = ((bf16[128,16,128]{2,1,0:T(8,128)(2,1)}), bf16[128,16,128]{2,1,0:T(8,128)(2,1)S(1)}, u32[]{:S(2)}, u32[]{:S(2)}) async-start(bf16[128,16,128]{2,1,0:T(8,128)(2,1)} %compress_range.1), calls=%async_computation | async-start | bytes 1048576 | tf_op jit(solution)/shard_map/all_to_all | solution.py:573
  15.2 3.0 %prepare.1 = (f32[4,8,128,128]{3,2,1,0:T(8,128)S(1)}, bf16[512,512]{1,0:T(8,128)(2,1)S(1)}, f32[2,24,128]{2,1,0:T(8,128)S(1)}) custom-call(bf16[512,2048]{1,0:T(8,128)(2,1)} %angle_hbm, f32[2,8,128,128]{3,2,1,0:T(8,128)} %constant.17.clone.twist_hbm, bf16[512,512]{1,0:T(8,128)(2,1)} %constant.18.clone.mats_hbm, f32[2,24,128]{2,1,0:T(8,128)} %constant.19.clone.last_hbm), custom_call_target="tpu_custom_call" | custom-call | flops 10000000 | bytes 8000000 | tf_op jit(solution)/shard_map/prepare/pallas_call | solution.py:266
  18.2 10.8 %all-to-all-done.lines = bf16[128,16,128]{2,1,0:T(8,128)(2,1)S(1)} async-done(((bf16[128,16,128]{2,1,0:T(8,128)(2,1)}), bf16[128,16,128]{2,1,0:T(8,128)(2,1)S(1)}, u32[]{:S(2)}, u32[]{:S(2)}) %all-to-all-start) | async-done | bytes 524320 | tf_op jit(solution)/shard_map/all_to_all | solution.py:573
  28.9 2.3 %focus_columns.1.image = bf16[2,64,2048]{2,1,0:T(8,128)(2,1)S(1)} custom-call(bf16[128,16,128]{2,1,0:T(8,128)(2,1)S(1)} %all-to-all-done.lines, f32[4,8,128,128]{3,2,1,0:T(8,128)S(1)} %get-tuple-element.19.factors, bf16[512,512]{1,0:T(8,128)(2,1)S(1)} %get-tuple-element.20.mats, f32[2,24,128]{2,1,0:T(8,128)S(1)} %get-tuple-element.21.last), custom_call_target="tpu_custom_call" | custom-call | flops 1000000000 | bytes 4000000 | tf_op jit(solution)/shard_map/focus_columns/pallas_call | solution.py:336
  31.3 0.8 %collective-permute-start.3 = (bf16[2,64,2048]{2,1,0:T(8,128)(2,1)S(1)}, bf16[2,64,2048]{2,1,0:T(8,128)(2,1)S(1)}, u32[]{:S(2)}, u32[]{:S(2)}) collective-permute-start(bf16[2,64,2048]{2,1,0:T(8,128)(2,1)S(1)} %focus_columns.1.image), channel_id=1, source_target_pairs={{0,2},{1,7},{2,4},{3,1},{4,6},{5,3},{6,0},{7,5},{8,10},{9,15},{10,... | collective-permute-start | bytes 1572872 | tf_op jit(solution)/shard_map/ppermute | solution.py:576
  32.1 1.3 %collective-permute-start = (bf16[2,64,2048]{2,1,0:T(8,128)(2,1)S(1)}, bf16[2,64,2048]{2,1,0:T(8,128)(2,1)S(1)}, u32[]{:S(2)}, u32[]{:S(2)}) collective-permute-start(bf16[2,64,2048]{2,1,0:T(8,128)(2,1)S(1)} %focus_columns.1.image), channel_id=1, source_target_pairs={{0,8},{1,9},{2,10},{3,11},{4,12},{5,13},{6,14},{7,15},{8,0},{9,1},... | collective-permute-start | bytes 1572872 | tf_op jit(solution)/shard_map/ppermute | solution.py:576
  33.3 0.2 collective-permute-start.1
  33.6 0.0 collective-permute-done.2.other
  33.6 7.6 %cross_first.1 = (f32[4,2,16,128]{3,2,1,0:T(8,128)S(1)}, bf16[4,2,192,2048]{3,2,1,0:T(8,128)(2,1)S(1)}, f32[3,4,16,128]{3,2,1,0:T(8,128)S(1)}, bf16[2048,128]{1,0:T(8,128)(2,1)S(1)}) custom-call(bf16[2,64,2048]{2,1,0:T(8,128)(2,1)S(1)} %focus_columns.1.image, bf16[2,2,512,2048]{3,2,1,0:T(8,128)(2,1)} %own, ...), custom_call_target="tpu_custom_call" | custom-call | flops 1000000000 | bytes 8000000 | tf_op jit(solution)/shard_map/cross_first/pallas_call | solution.py:433
  41.2 1.2 %collective-permute-done.3.image = bf16[2,64,2048]{2,1,0:T(8,128)(2,1)S(1)} collective-permute-done((bf16[2,64,2048]{2,1,0:T(8,128)(2,1)S(1)}, bf16[2,64,2048]{2,1,0:T(8,128)(2,1)S(1)}, u32[]{:S(2)}, u32[]{:S(2)}) %collective-permute-start.3) | collective-permute-done | bytes 524320 | tf_op jit(solution)/shard_map/ppermute | solution.py:576
  42.4 0.8 %cross_block.1.part1 = f32[4,2,16,128]{3,2,1,0:T(8,128)S(1)} custom-call(bf16[2,64,2048]{2,1,0:T(8,128)(2,1)S(1)} %collective-permute-done.3.image, bf16[4,2,192,2048]{3,2,1,0:T(8,128)(2,1)S(1)} %get-tuple-element.23.held, f32[3,4,16,128]{3,2,1,0:T(8,128)S(1)} %get-tuple-element.24.old_scales, bf16[2048,128]{1,0:T(8,128)(2,1)S(1)} %get-tuple-element.25.pooling), custom_call_target="tpu_custom_call" | custom-call | flops 100000000 | bytes 4000000 | tf_op jit(solution)/shard_map/cross_block/pallas_call | solution.py:463
  43.2 3.3 %collective-permute-done.image1 = bf16[2,64,2048]{2,1,0:T(8,128)(2,1)S(1)} collective-permute-done((bf16[2,64,2048]{2,1,0:T(8,128)(2,1)S(1)}, bf16[2,64,2048]{2,1,0:T(8,128)(2,1)S(1)}, u32[]{:S(2)}, u32[]{:S(2)}) %collective-permute-start) | collective-permute-done | bytes 524320 | tf_op jit(solution)/shard_map/ppermute | solution.py:576
  46.5 0.9 %collective-permute-done.1.image2 = bf16[2,64,2048]{2,1,0:T(8,128)(2,1)S(1)} collective-permute-done((bf16[2,64,2048]{2,1,0:T(8,128)(2,1)S(1)}, bf16[2,64,2048]{2,1,0:T(8,128)(2,1)S(1)}, u32[]{:S(2)}, u32[]{:S(2)}) %collective-permute-start.1) | collective-permute-done | bytes 524320 | tf_op jit(solution)/shard_map/ppermute | solution.py:576
  47.4 0.0 copy-start
  47.4 0.9 %cross_others.1 = (f32[2,2,64,128]{3,2,1,0:T(8,128)S(1)}, f32[2,16,128]{2,1,0:T(8,128)S(1)}) custom-call(bf16[2,64,2048]{2,1,0:T(8,128)(2,1)S(1)} %collective-permute-done.image1, bf16[2,64,2048]{2,1,0:T(8,128)(2,1)S(1)} %collective-permute-done.1.image2, bf16[4,2,192,2048]{3,2,1,0:T(8,128)(2,1)S(1)} %get-tuple-element.23.held, ...), custom_call_target="tpu_custom_call" | custom-call | flops 100000000 | bytes 4000000 | tf_op jit(solution)/shard_map/cross_others/pallas_call | solution.py:494
  48.3 0.6 %collective-permute-start.4 = (f32[2,2,64,128]{3,2,1,0:T(8,128)S(1)}, f32[2,2,64,128]{3,2,1,0:T(8,128)S(1)}, u32[]{:S(2)}, u32[]{:S(2)}) collective-permute-start(f32[2,2,64,128]{3,2,1,0:T(8,128)S(1)} %get-tuple-element.28), channel_id=1, source_target_pairs={{0,1},{1,0},{2,3},{3,2},{4,5},{5,4},{6,7},{7,6},{8,9},{9,8},{10,11... | collective-permute-start | bytes 393224 | tf_op jit(solution)/shard_map/ppermute | solution.py:580
  48.9 0.8 %cross_own.1.mine = f32[2,2,64,128]{3,2,1,0:T(8,128)S(1)} custom-call(bf16[2,64,2048]{2,1,0:T(8,128)(2,1)S(1)} %collective-permute-done.image1, bf16[2,64,2048]{2,1,0:T(8,128)(2,1)S(1)} %collective-permute-done.1.image2, bf16[4,2,192,2048]{3,2,1,0:T(8,128)(2,1)S(1)} %get-tuple-element.23.held, f32[3,4,16,128]{3,2,1,0:T(8,128)S(1)} %get-tuple-element.24.old_scales, ...), custom_call_target="tpu_custom_call" | custom-call | flops 100000000 | bytes 4000000 | tf_op jit(solution)/shard_map/cross_own/pallas_call | solution.py:519
  49.7 0.2 collective-permute-done.4.received
  49.9 0.0 copy-done
  49.9 0.7 %assemble.1 = f32[2,2,128,128]{3,2,1,0:T(8,128)} custom-call(s32[1,128]{1,0:T(1,128)S(1)} %broadcast_in_dim.3.order, f32[2,2,64,128]{3,2,1,0:T(8,128)S(1)} %cross_own.1.mine, f32[2,2,64,128]{3,2,1,0:T(8,128)S(1)} %collective-permute-done.4.received), custom_call_target="tpu_custom_call" | custom-call | flops 1000000 | bytes 1000000 | tf_op jit(solution)/shard_map/assemble/pallas_call | solution.py:543
  (1 shorter events, 0.0 us)
Async XLA Ops:
  3.5 30.1 %collective-permute-start.2 = (bf16[2,2,512,2048]{3,2,1,0:T(8,128)(2,1)}, bf16[2,2,512,2048]{3,2,1,0:T(8,128)(2,1)}, u32[]{:S(2)}, u32[]{:S(2)}) collective-permute-start(bf16[2,2,512,2048]{3,2,1,0:T(8,128)(2,1)} %own), channel_id=1, source_target_pairs={{0,1},{1,0},{2,3},{3,2},{4,5},{5,4},{6,7},{7,6},{8,9},{9,8},{10,11... | collective-permute-start | bytes 25165832 | tf_op jit(solution)/shard_map/ppermute | solution.py:574
  5.0 24.0 %all-to-all-start = ((bf16[128,16,128]{2,1,0:T(8,128)(2,1)}), bf16[128,16,128]{2,1,0:T(8,128)(2,1)S(1)}, u32[]{:S(2)}, u32[]{:S(2)}) async-start(bf16[128,16,128]{2,1,0:T(8,128)(2,1)} %compress_range.1), calls=%async_computation | async-start | bytes 1048576 | tf_op jit(solution)/shard_map/all_to_all | solution.py:573
  31.3 11.1 %collective-permute-start.3 = (bf16[2,64,2048]{2,1,0:T(8,128)(2,1)S(1)}, bf16[2,64,2048]{2,1,0:T(8,128)(2,1)S(1)}, u32[]{:S(2)}, u32[]{:S(2)}) collective-permute-start(bf16[2,64,2048]{2,1,0:T(8,128)(2,1)S(1)} %focus_columns.1.image), channel_id=1, source_target_pairs={{0,2},{1,7},{2,4},{3,1},{4,6},{5,3},{6,0},{7,5},{8,10},{9,15},{10,... | collective-permute-start | bytes 1572872 | tf_op jit(solution)/shard_map/ppermute | solution.py:576
  32.1 14.5 %collective-permute-start = (bf16[2,64,2048]{2,1,0:T(8,128)(2,1)S(1)}, bf16[2,64,2048]{2,1,0:T(8,128)(2,1)S(1)}, u32[]{:S(2)}, u32[]{:S(2)}) collective-permute-start(bf16[2,64,2048]{2,1,0:T(8,128)(2,1)S(1)} %focus_columns.1.image), channel_id=1, source_target_pairs={{0,8},{1,9},{2,10},{3,11},{4,12},{5,13},{6,14},{7,15},{8,0},{9,1},... | collective-permute-start | bytes 1572872 | tf_op jit(solution)/shard_map/ppermute | solution.py:576
  33.3 14.1 %collective-permute-start.1 = (bf16[2,64,2048]{2,1,0:T(8,128)(2,1)S(1)}, bf16[2,64,2048]{2,1,0:T(8,128)(2,1)S(1)}, u32[]{:S(2)}, u32[]{:S(2)}) collective-permute-start(bf16[2,64,2048]{2,1,0:T(8,128)(2,1)S(1)} %focus_columns.1.image), channel_id=1, source_target_pairs={{0,6},{1,3},{2,0},{3,5},{4,2},{5,7},{6,4},{7,1},{8,14},{9,11},{10,... | collective-permute-start | bytes 1572872 | tf_op jit(solution)/shard_map/ppermute | solution.py:576
  47.4 2.5 %copy-start = (s32[2]{0:T(128)S(1)}, s32[2]{0:T(128)}, u32[]{:S(2)}) copy-start(s32[2]{0:T(128)} %param.16) | copy-start | bytes 28
  48.3 1.6 %collective-permute-start.4 = (f32[2,2,64,128]{3,2,1,0:T(8,128)S(1)}, f32[2,2,64,128]{3,2,1,0:T(8,128)S(1)}, u32[]{:S(2)}, u32[]{:S(2)}) collective-permute-start(f32[2,2,64,128]{3,2,1,0:T(8,128)S(1)} %get-tuple-element.28), channel_id=1, source_target_pairs={{0,1},{1,0},{2,3},{3,2},{4,5},{5,4},{6,7},{7,6},{8,9},{9,8},{10,11... | collective-permute-start | bytes 393224 | tf_op jit(solution)/shard_map/ppermute | solution.py:580

commit v5 on v3

--- a/solution.py
+++ b/solution.py
@@ -539,7 +539,7 @@
             out[1, part, rows, :] = jnp.where(odd_first, even, odd)
 
 
-def assemble(date_order, mine, received):
+def assemble(order_row, mine, received):
     return pl.pallas_call(
         final_kernel,
         out_shape=jax.ShapeDtypeStruct((2, 2, 128, 128), F32),
@@ -548,7 +548,7 @@
         compiler_params=params(24),
         cost_estimate=cost(10**6, 10**6),
         name="assemble",
-    )(jnp.broadcast_to(date_order[0], (1, 128)), mine, received)
+    )(order_row, mine, received)
 
 
 def pairs(step):
@@ -573,11 +573,12 @@
     image = focus_columns(lines, *prepare(azimuth_phase))
     images = [lax.ppermute(image, "date", perm) for perm in (NEXT_Y, OTHER_Z, LAST_Y)]
     first, *kept = cross_first(image, archive, other_archive, jnp.asarray(pooling_table()))
+    first, order_row = lax.optimization_barrier((first, jnp.broadcast_to(date_order[0], (1, 128))))
     parts = [first, cross_block(0, images[0], *kept)]
     others, new_scale = cross_others(images[1:], *kept, parts)
     received = lax.ppermute(others, "date", OTHER_CORE)
     mine = cross_own(images[1:], *kept, parts, new_scale)
-    return assemble(date_order, mine, received)
+    return assemble(order_row, mine, received)
 
 
 def solution(mesh):

time: 50.7 us -> 50.7 us (level)
  no operation moved by 1% of the time
where the time goes in v5:
time: 50.7 us; the launch traced here: 50.5 us
  Pallas kernels  19.6 us (39%)
  starting transfers between devices  16.6 us (33%)
  waiting for transfers between devices  14.1 us (28%)
    all_to_all x1, waiting for transfers between devices, on_device(): lines = lax.all_to_all(messages, ALL, 0, 0, tiled=True)  10.8 us
    all_to_all x1, starting transfers between devices, on_device(): lines = lax.all_to_all(messages, ALL, 0, 0, tiled=True)  10.2 us
    pallas_call x1, Pallas kernels, cross_first(): pl.pallas_call(first_kernel, out_shape=(jax.ShapeDtypeStruct((4, 2, 16, 1...  7.6 us
    ppermute x3, starting transfers between devices, on_device(): lax.ppermute(image, 'date', perm)  3.51 us
    pallas_call x1, Pallas kernels, compress_range(): pl.pallas_call(range_kernel, out_shape=jax.ShapeDtypeStruct((128, 16, 128...  3.44 us
    ppermute x3, waiting for transfers between devices, on_device(): lax.ppermute(image, 'date', perm)  3.16 us
    pallas_call x1, Pallas kernels, prepare(): pl.pallas_call(prepare_kernel, out_shape=(pltpu.VMEM((4, 8, 128, 128), F3...  3 us
    pallas_call x1, Pallas kernels, focus_columns(): pl.pallas_call(focus_kernel, out_shape=jax.ShapeDtypeStruct((2, ROWS, A),...  2.35 us
  transfers between devices with their start and end apart: 6, of which 3 were waited for; matrix products, arithmetic and copies ran while one was open for 0% of the time, Pallas kernels for 29%

profile of v5, /device:TPU:1, one launch (start us, length us, event | category | flops | bytes accessed | tf_op | source)
XLA Modules:
  0.0 50.5 jit_solution(8650260493075570110)
XLA Ops:
  0.0 3.4 %compress_range.1 = bf16[128,16,128]{2,1,0:T(8,128)(2,1)} custom-call(bf16[2,16,4096]{2,1,0:T(8,128)(2,1)} %raw_hbm.1, f32[32,128]{1,0:T(8,128)} %bitcast.3, f32[2,32,128]{2,1,0:T(8,128)} %constant.14.clone.twist_hbm, bf16[768,256]{1,0:T(8,128)(2,1)} %constant.15.clone.fwd_hbm, bf16[768,256]{1,0:T(8,128)(2,1)} %constant.16.clone.bwd_hbm), custom_call_target="tpu_custom_call" | custom-call | flops 400000000 | bytes 2000000 | tf_op jit(solution)/shard_map/compress_range/pallas_call | solution.py:224
  3.5 1.5 %collective-permute-start = (bf16[2,2,512,2048]{3,2,1,0:T(8,128)(2,1)}, bf16[2,2,512,2048]{3,2,1,0:T(8,128)(2,1)}, u32[]{:S(2)}, u32[]{:S(2)}) collective-permute-start(bf16[2,2,512,2048]{3,2,1,0:T(8,128)(2,1)} %own), channel_id=1, source_target_pairs={{0,1},{1,0},{2,3},{3,2},{4,5},{5,4},{6,7},{7,6},{8,9},{9,8},{10,11... | collective-permute-start | bytes 25165832 | tf_op jit(solution)/shard_map/ppermute | solution.py:572
  5.0 10.2 %all-to-all-start = ((bf16[128,16,128]{2,1,0:T(8,128)(2,1)}), bf16[128,16,128]{2,1,0:T(8,128)(2,1)S(1)}, u32[]{:S(2)}, u32[]{:S(2)}) async-start(bf16[128,16,128]{2,1,0:T(8,128)(2,1)} %compress_range.1), calls=%async_computation | async-start | bytes 1048576 | tf_op jit(solution)/shard_map/all_to_all | solution.py:571
  15.2 3.0 %prepare.1 = (f32[4,8,128,128]{3,2,1,0:T(8,128)S(1)}, bf16[512,512]{1,0:T(8,128)(2,1)S(1)}, f32[2,24,128]{2,1,0:T(8,128)S(1)}) custom-call(bf16[512,2048]{1,0:T(8,128)(2,1)} %angle_hbm, f32[2,8,128,128]{3,2,1,0:T(8,128)} %constant.17.clone.twist_hbm, bf16[512,512]{1,0:T(8,128)(2,1)} %constant.18.clone.mats_hbm, f32[2,24,128]{2,1,0:T(8,128)} %constant.19.clone.last_hbm), custom_call_target="tpu_custom_call" | custom-call | flops 10000000 | bytes 8000000 | tf_op jit(solution)/shard_map/prepare/pallas_call | solution.py:266
  18.2 10.8 %all-to-all-done.lines = bf16[128,16,128]{2,1,0:T(8,128)(2,1)S(1)} async-done(((bf16[128,16,128]{2,1,0:T(8,128)(2,1)}), bf16[128,16,128]{2,1,0:T(8,128)(2,1)S(1)}, u32[]{:S(2)}, u32[]{:S(2)}) %all-to-all-start) | async-done | bytes 524320 | tf_op jit(solution)/shard_map/all_to_all | solution.py:571
  28.9 2.3 %focus_columns.1.image = bf16[2,64,2048]{2,1,0:T(8,128)(2,1)S(1)} custom-call(bf16[128,16,128]{2,1,0:T(8,128)(2,1)S(1)} %all-to-all-done.lines, f32[4,8,128,128]{3,2,1,0:T(8,128)S(1)} %get-tuple-element.21.factors, bf16[512,512]{1,0:T(8,128)(2,1)S(1)} %get-tuple-element.22.mats, f32[2,24,128]{2,1,0:T(8,128)S(1)} %get-tuple-element.23.last), custom_call_target="tpu_custom_call" | custom-call | flops 1000000000 | bytes 4000000 | tf_op jit(solution)/shard_map/focus_columns/pallas_call | solution.py:336
  31.3 0.0 copy-start
  31.3 0.4 collective-permute-start.3
  31.7 0.5 %collective-permute-start.1 = (bf16[2,64,2048]{2,1,0:T(8,128)(2,1)S(1)}, bf16[2,64,2048]{2,1,0:T(8,128)(2,1)S(1)}, u32[]{:S(2)}, u32[]{:S(2)}) collective-permute-start(bf16[2,64,2048]{2,1,0:T(8,128)(2,1)S(1)} %focus_columns.1.image), channel_id=1, source_target_pairs={{0,8},{1,9},{2,10},{3,11},{4,12},{5,13},{6,14},{7,15},{8,0},{9,1},... | collective-permute-start | bytes 1572872 | tf_op jit(solution)/shard_map/ppermute | solution.py:574
  32.2 2.6 %collective-permute-start.2 = (bf16[2,64,2048]{2,1,0:T(8,128)(2,1)S(1)}, bf16[2,64,2048]{2,1,0:T(8,128)(2,1)S(1)}, u32[]{:S(2)}, u32[]{:S(2)}) collective-permute-start(bf16[2,64,2048]{2,1,0:T(8,128)(2,1)S(1)} %focus_columns.1.image), channel_id=1, source_target_pairs={{0,6},{1,7},{2,0},{3,1},{4,2},{5,3},{6,4},{7,5},{8,14},{9,15},{10,... | collective-permute-start | bytes 1572872 | tf_op jit(solution)/shard_map/ppermute | solution.py:574
  34.8 0.0 collective-permute-done.other
  34.8 7.6 %cross_first.1 = (f32[4,2,16,128]{3,2,1,0:T(8,128)S(1)}, bf16[4,2,192,2048]{3,2,1,0:T(8,128)(2,1)S(1)}, f32[3,4,16,128]{3,2,1,0:T(8,128)S(1)}, bf16[2048,128]{1,0:T(8,128)(2,1)S(1)}) custom-call(bf16[2,64,2048]{2,1,0:T(8,128)(2,1)S(1)} %focus_columns.1.image, bf16[2,2,512,2048]{3,2,1,0:T(8,128)(2,1)} %own, ...), custom_call_target="tpu_custom_call" | custom-call | flops 1000000000 | bytes 8000000 | tf_op jit(solution)/shard_map/cross_first/pallas_call | solution.py:433
  42.4 0.0 copy-done
  42.5 3.2 %collective-permute-done.3.image = bf16[2,64,2048]{2,1,0:T(8,128)(2,1)S(1)} collective-permute-done((bf16[2,64,2048]{2,1,0:T(8,128)(2,1)S(1)}, bf16[2,64,2048]{2,1,0:T(8,128)(2,1)S(1)}, u32[]{:S(2)}, u32[]{:S(2)}) %collective-permute-start.3) | collective-permute-done | bytes 524320 | tf_op jit(solution)/shard_map/ppermute | solution.py:574
  45.6 0.8 %cross_block.1.part1 = f32[4,2,16,128]{3,2,1,0:T(8,128)S(1)} custom-call(bf16[2,64,2048]{2,1,0:T(8,128)(2,1)S(1)} %collective-permute-done.3.image, bf16[4,2,192,2048]{3,2,1,0:T(8,128)(2,1)S(1)} %get-tuple-element.27.held, f32[3,4,16,128]{3,2,1,0:T(8,128)S(1)} %get-tuple-element.28.old_scales, bf16[2048,128]{1,0:T(8,128)(2,1)S(1)} %get-tuple-element.29.pooling), custom_call_target="tpu_custom_call" | custom-call | flops 100000000 | bytes 4000000 | tf_op jit(solution)/shard_map/cross_block/pallas_call | solution.py:463
  46.5 0.0 collective-permute-done.1.image1
  46.5 0.0 collective-permute-done.2.image2
  46.5 0.9 %cross_others.1 = (f32[2,2,64,128]{3,2,1,0:T(8,128)S(1)}, f32[2,16,128]{2,1,0:T(8,128)S(1)}) custom-call(bf16[2,64,2048]{2,1,0:T(8,128)(2,1)S(1)} %collective-permute-done.1.image1, bf16[2,64,2048]{2,1,0:T(8,128)(2,1)S(1)} %collective-permute-done.2.image2, bf16[4,2,192,2048]{3,2,1,0:T(8,128)(2,1)S(1)} %get-tuple-element.27.held, ...), custom_call_target="tpu_custom_call" | custom-call | flops 100000000 | bytes 4000000 | tf_op jit(solution)/shard_map/cross_others/pallas_call | solution.py:494
  47.4 1.4 %collective-permute-start.4 = (f32[2,2,64,128]{3,2,1,0:T(8,128)S(1)}, f32[2,2,64,128]{3,2,1,0:T(8,128)S(1)}, u32[]{:S(2)}, u32[]{:S(2)}) collective-permute-start(f32[2,2,64,128]{3,2,1,0:T(8,128)S(1)} %get-tuple-element.32), channel_id=1, source_target_pairs={{0,1},{1,0},{2,3},{3,2},{4,5},{5,4},{6,7},{7,6},{8,9},{9,8},{10,11... | collective-permute-start | bytes 393224 | tf_op jit(solution)/shard_map/ppermute | solution.py:579
  48.7 0.8 %cross_own.1.mine = f32[2,2,64,128]{3,2,1,0:T(8,128)S(1)} custom-call(bf16[2,64,2048]{2,1,0:T(8,128)(2,1)S(1)} %collective-permute-done.1.image1, bf16[2,64,2048]{2,1,0:T(8,128)(2,1)S(1)} %collective-permute-done.2.image2, bf16[4,2,192,2048]{3,2,1,0:T(8,128)(2,1)S(1)} %get-tuple-element.27.held, f32[3,4,16,128]{3,2,1,0:T(8,128)S(1)} %get-tuple-element.28.old_scales, ...), custom_call_target="tpu_custom_call" | custom-call | flops 100000000 | bytes 4000000 | tf_op jit(solution)/shard_map/cross_own/pallas_call | solution.py:519
  49.5 0.2 collective-permute-done.4.received
  49.7 0.7 %assemble.1 = f32[2,2,128,128]{3,2,1,0:T(8,128)} custom-call(s32[1,128]{1,0:T(1,128)S(1)} %broadcast_in_dim.3.order, f32[2,2,64,128]{3,2,1,0:T(8,128)S(1)} %cross_own.1.mine, f32[2,2,64,128]{3,2,1,0:T(8,128)S(1)} %collective-permute-done.4.received), custom_call_target="tpu_custom_call" | custom-call | flops 1000000 | bytes 1000000 | tf_op jit(solution)/shard_map/assemble/pallas_call | solution.py:543
  (1 shorter events, 0.0 us)
Async XLA Ops:
  3.5 31.4 %collective-permute-start = (bf16[2,2,512,2048]{3,2,1,0:T(8,128)(2,1)}, bf16[2,2,512,2048]{3,2,1,0:T(8,128)(2,1)}, u32[]{:S(2)}, u32[]{:S(2)}) collective-permute-start(bf16[2,2,512,2048]{3,2,1,0:T(8,128)(2,1)} %own), channel_id=1, source_target_pairs={{0,1},{1,0},{2,3},{3,2},{4,5},{5,4},{6,7},{7,6},{8,9},{9,8},{10,11... | collective-permute-start | bytes 25165832 | tf_op jit(solution)/shard_map/ppermute | solution.py:572
  5.0 24.0 %all-to-all-start = ((bf16[128,16,128]{2,1,0:T(8,128)(2,1)}), bf16[128,16,128]{2,1,0:T(8,128)(2,1)S(1)}, u32[]{:S(2)}, u32[]{:S(2)}) async-start(bf16[128,16,128]{2,1,0:T(8,128)(2,1)} %compress_range.1), calls=%async_computation | async-start | bytes 1048576 | tf_op jit(solution)/shard_map/all_to_all | solution.py:571
  31.3 11.1 %copy-start = (s32[2]{0:T(128)S(1)}, s32[2]{0:T(128)}, u32[]{:S(2)}) copy-start(s32[2]{0:T(128)} %param.16) | copy-start | bytes 28
  31.3 14.3 %collective-permute-start.3 = (bf16[2,64,2048]{2,1,0:T(8,128)(2,1)S(1)}, bf16[2,64,2048]{2,1,0:T(8,128)(2,1)S(1)}, u32[]{:S(2)}, u32[]{:S(2)}) collective-permute-start(bf16[2,64,2048]{2,1,0:T(8,128)(2,1)S(1)} %focus_columns.1.image), channel_id=1, source_target_pairs={{0,2},{1,3},{2,4},{3,5},{4,6},{5,7},{6,0},{7,1},{8,10},{9,11},{10,... | collective-permute-start | bytes 1572872 | tf_op jit(solution)/shard_map/ppermute | solution.py:574
  31.7 14.7 %collective-permute-start.1 = (bf16[2,64,2048]{2,1,0:T(8,128)(2,1)S(1)}, bf16[2,64,2048]{2,1,0:T(8,128)(2,1)S(1)}, u32[]{:S(2)}, u32[]{:S(2)}) collective-permute-start(bf16[2,64,2048]{2,1,0:T(8,128)(2,1)S(1)} %focus_columns.1.image), channel_id=1, source_target_pairs={{0,8},{1,9},{2,10},{3,11},{4,12},{5,13},{6,14},{7,15},{8,0},{9,1},... | collective-permute-start | bytes 1572872 | tf_op jit(solution)/shard_map/ppermute | solution.py:574
  32.2 14.2 %collective-permute-start.2 = (bf16[2,64,2048]{2,1,0:T(8,128)(2,1)S(1)}, bf16[2,64,2048]{2,1,0:T(8,128)(2,1)S(1)}, u32[]{:S(2)}, u32[]{:S(2)}) collective-permute-start(bf16[2,64,2048]{2,1,0:T(8,128)(2,1)S(1)} %focus_columns.1.image), channel_id=1, source_target_pairs={{0,6},{1,7},{2,0},{3,1},{4,2},{5,3},{6,4},{7,5},{8,14},{9,15},{10,... | collective-permute-start | bytes 1572872 | tf_op jit(solution)/shard_map/ppermute | solution.py:574
  47.4 2.4 %collective-permute-start.4 = (f32[2,2,64,128]{3,2,1,0:T(8,128)S(1)}, f32[2,2,64,128]{3,2,1,0:T(8,128)S(1)}, u32[]{:S(2)}, u32[]{:S(2)}) collective-permute-start(f32[2,2,64,128]{3,2,1,0:T(8,128)S(1)} %get-tuple-element.32), channel_id=1, source_target_pairs={{0,1},{1,0},{2,3},{3,2},{4,5},{5,4},{6,7},{7,6},{8,9},{9,8},{10,11... | collective-permute-start | bytes 393224 | tf_op jit(solution)/shard_map/ppermute | solution.py:579
